TPU v7x, 32 devices: a whole 2x2x4 slice. The times are simulated.
32 devices in a mesh: gx: 16 (over z, y, x), gy: 2 (over core).
Axes of the slice: x: 2, y: 2, z: 4, core: 2. Of those that a mesh axis runs over, the one named last changes fastest.
Arguments:
- velocity: float32 [384, 8, 512], P('gx', None, 'gy'), may hold values from -6 to 6
- viscosity: float32 [384, 8, 512], P('gx', None, 'gy'), may hold values from 0.5 to 4
- explicit: float32 [384, 8, 512], P('gx', None, 'gy'), may hold values from -60 to 60
Outputs:
- updated: float32 [384, 8, 512], P('gx', None, 'gy')
All inputs are finite; a program needn't handle non-finite values.
Results may differ from a plain program's by a relative error of at most 0.0003.
Values sent between devices are 32-bit elements; how exact they have to be, the bound alone decides.
No kernel may reach another device: no remote copies, remote signals or barrier semaphores. Data moves between devices by JAX's collectives and lax.ppermute only.
A program may use at most 128 MiB of HBM per device.

v0:
```python
import jax
import jax.numpy as jnp
from jax import lax
from jax.experimental import pallas as pl
from jax.experimental.pallas import tpu as pltpu
from jax.sharding import PartitionSpec as P

stream_rate = 1000.0
normal_rate = 50.0


def merge(a, b):
    oa, sla, sra, rla, rra = a
    ob, slb, srb, rlb, rrb = b
    sm = slb if sra is None else sra + slb
    rm = rlb if rra is None else rra + rlb
    t = 1.0 / (oa + ob + sm)
    ga = oa * t
    gb = ob * t
    gsb = gb * sm
    grb = gb * rm
    block = (
        oa * gb,
        sla + ga * sm,
        gsb if srb is None else srb + gsb,
        rla + ga * rm,
        grb if rrb is None else rrb + grb,
    )
    return block, (t * rm, ga, gb)


def tree_up(blocks):
    levels = []
    while len(blocks) > 1:
        joined, joints = [], []
        for i in range(0, len(blocks) - 1, 2):
            block, joint = merge(blocks[i], blocks[i + 1])
            joined.append(block)
            joints.append(joint)
        if len(blocks) % 2:
            joined.append(blocks[-1])
        levels.append((len(blocks), joints))
        blocks = joined
    return blocks[0], levels


def level_sizes(count):
    sizes = []
    while count > 1:
        sizes.append(count)
        count = (count + 1) // 2
    return sizes


def wall_kernel(v_ref, c_ref, e_ref, h_ref, base_ref, g_ref, edge_ref):
    rows, planes, width = v_ref.shape
    upper = lax.axis_index("gy") == 1
    lane = lax.broadcasted_iota(jnp.int32, (planes, width), 1)
    last = lane == width - 1
    first = lane == 0
    at_wall = (last & upper) | (first & jnp.logical_not(upper))
    at_joint = (first & upper) | (last & jnp.logical_not(upper))
    unit = jnp.where(at_joint, 1.0, 0.0)
    lane_out = lax.broadcasted_iota(jnp.int32, (planes, 128), 1)

    def vel(i):
        return h_ref[i + 2] if i < 0 else v_ref[i]

    def visc(i):
        return h_ref[i + 4] if i < 0 else c_ref[i]

    def expl(i):
        return h_ref[4] if i < 0 else e_ref[i]

    for i in range(-1, rows - 1):
        v = vel(i)
        c = visc(i)
        east = 0.5 * stream_rate * (c + visc(i + 1))
        west = 0.5 * stream_rate * (c + visc(i - 1))
        lap = east * (vel(i + 1) - v) - west * (v - vel(i - 1))
        r = v + lap + expl(i)
        o = jnp.where(last, 0.0, 0.5 * normal_rate * (c + pltpu.roll(c, width - 1, 1)))
        d = 1.0 + o + pltpu.roll(o, 1, 1) + jnp.where(at_wall, normal_rate * c, 0.0)
        g = unit
        h = 1
        while h < width:
            t = 1.0 / d
            u = o * t
            w = o * pltpu.roll(t, width - h, 1)
            r_new = r + pltpu.roll(u * r, h, 1) + o * pltpu.roll(t * r, width - h, 1)
            g_new = g + pltpu.roll(u * g, h, 1) + o * pltpu.roll(t * g, width - h, 1)
            d = d - pltpu.roll(o * u, h, 1) - o * w
            o = w * pltpu.roll(o, width - h, 1)
            r, g = r_new, g_new
            h *= 2
        t = 1.0 / d
        base = r * t
        g = g * t
        base_ref[i + 1] = base - lap
        g_ref[i + 1] = g

        def edge(x):
            return jnp.sum(x * unit, axis=1, keepdims=True)

        edge_ref[i + 1] = jnp.where(
            lane_out == 0, edge(base), jnp.where(lane_out == 1, edge(g), edge(c))
        )


def reduce_kernel(c_ref, h_ref, base_ref, g_ref, mine_ref, theirs_ref, block_ref, joint_ref):
    rows, planes, width = c_ref.shape

    def visc(i):
        return h_ref[i + 4] if i < 0 else c_ref[i]

    blocks = []
    for r in range(rows):
        b0 = mine_ref[r, :, 0:1]
        g0 = mine_ref[r, :, 1:2]
        c0 = mine_ref[r, :, 2:3]
        b1 = theirs_ref[r, :, 0:1]
        g1 = theirs_ref[r, :, 1:2]
        c1 = theirs_ref[r, :, 2:3]
        face = 0.5 * normal_rate * (c0 + c1)
        flux = face * (b1 - b0) / (1.0 + face * (g0 + g1))
        q = base_ref[r] + flux * g_ref[r]
        o = 0.5 * stream_rate * (visc(r - 1) + visc(r))
        blocks.append((o, jnp.ones_like(q), None, q, None))
    whole, levels = tree_up(blocks)
    for n in range(5):
        block_ref[n] = whole[n]
    at = 0
    for _, joints in levels:
        for joint in joints:
            for n in range(3):
                joint_ref[at, n] = joint[n]
            at += 1


def finish_kernel(joint_ref, ends_ref, out_ref):
    rows = out_ref.shape[0]
    sizes = level_sizes(rows)
    starts = []
    at = 0
    for s in sizes:
        starts.append(at)
        at += s // 2
    ends = [ends_ref[0], ends_ref[1]]
    for s, start in reversed(list(zip(sizes, starts))):
        new = []
        for i in range(s // 2):
            left, right = ends[i], ends[i + 1]
            at = start + i
            mid = joint_ref[at, 0] + joint_ref[at, 1] * left + joint_ref[at, 2] * right
            new += [left, mid]
        new += ends[s // 2 :]
        ends = new
    for i in range(rows):
        out_ref[i] = ends[i + 1]


def per_device(velocity, viscosity, explicit):
    rows, planes, width = velocity.shape
    f32 = jnp.float32
    count = lax.axis_size("gx")
    tail = jnp.concatenate([velocity[-2:], viscosity[-2:], explicit[-1:]], axis=0)
    halo = lax.ppermute(tail, "gx", [(i, (i + 1) % count) for i in range(count)])
    shape = jax.ShapeDtypeStruct((rows, planes, width), f32)
    base, g, edge = pl.pallas_call(
        wall_kernel,
        out_shape=[shape, shape, jax.ShapeDtypeStruct((rows, planes, 128), f32)],
        name="wall",
    )(velocity, viscosity, explicit, halo)
    other = lax.ppermute(edge, "gy", [(0, 1), (1, 0)])
    block, joints = pl.pallas_call(
        reduce_kernel,
        out_shape=[
            jax.ShapeDtypeStruct((5, planes, width), f32),
            jax.ShapeDtypeStruct((rows - 1, 3, planes, width), f32),
        ],
        name="reduce",
    )(viscosity, halo, base, g, edge, other)
    rank = lax.axis_index("gx")
    path = []
    bit = 1
    while bit < count:
        partner = lax.ppermute(block, "gx", [(i, i ^ bit) for i in range(count)])
        right = (rank & bit) != 0
        a = jnp.where(right, partner, block)
        b = jnp.where(right, block, partner)
        whole, joint = merge(tuple(a[n] for n in range(5)), tuple(b[n] for n in range(5)))
        path.append((right, joint))
        block = jnp.stack(whole)
        bit *= 2
    top = (block[3] + block[4]) / (block[1] + block[2])
    low, high = top, top
    for right, (z, ga, gb) in reversed(path):
        mid = z + ga * low + gb * high
        low, high = jnp.where(right, mid, low), jnp.where(right, high, mid)
    ends = jnp.stack([low, high])
    return pl.pallas_call(finish_kernel, out_shape=shape, name="finish")(joints, ends)


def solution(mesh):
    return jax.shard_map(
        per_device,
        mesh=mesh,
        in_specs=(P("gx", None, "gy"), P("gx", None, "gy"), P("gx", None, "gy")),
        out_specs=P("gx", None, "gy"),
        check_vma=False,
    )
```

profile of v0, /device:TPU:0, one launch (start us, length us, event | category | flops | bytes accessed | tf_op | source)
XLA Modules:
  0.0 51.8 jit_solution(4197942524023074002)
XLA Ops:
  0.0 0.0 slice-start
  0.0 0.0 slice-start.1
  0.0 0.0 slice-start.2
  0.0 0.7 %slice-done = f32[2,8,256]{2,1,0:T(8,128)S(1)} async-done(((f32[24,8,256]{2,1,0:T(8,128)}), f32[2,8,256]{2,1,0:T(8,128)S(1)}, s32[]{:S(2)}) %slice-start) | async-done | bytes 16408 | tf_op jit(solution)/shard_map/slice | solution.py:166
  0.7 0.0 slice-done.1
  0.7 0.0 slice-done.2
  0.7 3.0 %collective-permute-start = (f32[5,8,256]{2,1,0:T(8,128)S(1)}, f32[5,8,256]{2,1,0:T(8,128)S(1)}, u32[]{:S(2)}, u32[]{:S(2)}) collective-permute-start(f32[5,8,256]{2,1,0:T(8,128)S(1)} %pad_maximum_fusion), channel_id=1, source_target_pairs={{0,2},{2,4},{4,6},{6,8},{8,10},{10,12},{12,14},{14,16},{16,18},{18... | collective-permute-start | bytes 122888 | tf_op jit(solution)/shard_map/ppermute | solution.py:167
  3.7 6.0 %collective-permute-done.h_ref = f32[5,8,256]{2,1,0:T(8,128)S(1)} collective-permute-done((f32[5,8,256]{2,1,0:T(8,128)S(1)}, f32[5,8,256]{2,1,0:T(8,128)S(1)}, u32[]{:S(2)}, u32[]{:S(2)}) %collective-permute-start) | collective-permute-done | bytes 40992 | tf_op jit(solution)/shard_map/ppermute | solution.py:167
  9.7 0.0 copy-start
  9.7 0.6 %copy-done = f32[5,8,256]{2,1,0:T(8,128)} copy-done((f32[5,8,256]{2,1,0:T(8,128)}, f32[5,8,256]{2,1,0:T(8,128)S(1)}, u32[]{:S(2)}) %copy-start) | copy-done | bytes 40984
  10.3 16.2 %wall.1 = (f32[24,8,256]{2,1,0:T(8,128)}, f32[24,8,256]{2,1,0:T(8,128)}, f32[24,8,128]{2,1,0:T(8,128)}) custom-call(f32[24,8,256]{2,1,0:T(8,128)} %v_ref.1, f32[24,8,256]{2,1,0:T(8,128)} %c_ref.3, f32[24,8,256]{2,1,0:T(8,128)} %e_ref.1, f32[5,8,256]{2,1,0:T(8,128)} %copy-done), custom_call_target="tpu_custom_call" | custom-call | tf_op jit(solution)/shard_map/wall/pallas_call | solution.py:169
  26.5 0.0 collective-permute-start.1
  26.5 1.5 %collective-permute-done.1.theirs_ref = f32[24,8,128]{2,1,0:T(8,128)S(1)} collective-permute-done((f32[24,8,128]{2,1,0:T(8,128)}, f32[24,8,128]{2,1,0:T(8,128)S(1)}, u32[]{:S(2)}, u32[]{:S(2)}) %collective-permute-start.1) | collective-permute-done | bytes 98336 | tf_op jit(solution)/shard_map/ppermute | solution.py:174
  28.0 0.0 copy-start.1
  28.0 0.6 %copy-done.1 = f32[24,8,128]{2,1,0:T(8,128)} copy-done((f32[24,8,128]{2,1,0:T(8,128)}, f32[24,8,128]{2,1,0:T(8,128)S(1)}, u32[]{:S(2)}) %copy-start.1) | copy-done | bytes 98328
  28.6 2.3 %reduce.1 = (f32[5,8,256]{2,1,0:T(8,128)}, f32[23,3,8,256]{3,2,1,0:T(8,128)}) custom-call(f32[24,8,256]{2,1,0:T(8,128)} %c_ref.3, f32[5,8,256]{2,1,0:T(8,128)} %copy-done, f32[24,8,256]{2,1,0:T(8,128)} %get-tuple-element.10.base_ref, f32[24,8,256]{2,1,0:T(8,128)} %get-tuple-element.11.g_ref, f32[24,8,128]{2,1,0:T(8,128)} %get-tuple-element.12.mine_ref, ...), custom_call_target="tpu_custom_call" | custom-call | tf_op jit(solution)/shard_map/reduce/pallas_call | solution.py:175
  30.9 0.0 collective-permute-start.2
  31.0 4.2 %collective-permute-done.2 = f32[5,8,256]{2,1,0:T(8,128)S(1)} collective-permute-done((f32[5,8,256]{2,1,0:T(8,128)}, f32[5,8,256]{2,1,0:T(8,128)S(1)}, u32[]{:S(2)}, u32[]{:S(2)}) %collective-permute-start.2) | collective-permute-done | bytes 40992 | tf_op jit(solution)/shard_map/ppermute | solution.py:187
  35.2 0.8 %broadcast_select_fusion.6 = (f32[5,8,256]{2,1,0:T(8,128)S(1)}, f32[5,8,256]{2,1,0:T(8,128)S(1)}) fusion(f32[5,8,256]{2,1,0:T(8,128)} %get-tuple-element.14, f32[5,8,256]{2,1,0:T(8,128)S(1)} %collective-permute-done.2, pred[]{:T(512)S(6)} %ne.12), kind=kLoop, calls=%fused_computation.22 | loop fusion | flops 20480 | bytes 163841 | tf_op jit(solution)/shard_map/jit(_where)/select_n | solution.py:190
  36.0 0.1 collective-permute-start.3
  36.1 4.0 %collective-permute-done.3 = f32[5,8,256]{2,1,0:T(8,128)S(1)} collective-permute-done((f32[5,8,256]{2,1,0:T(8,128)S(1)}, f32[5,8,256]{2,1,0:T(8,128)S(1)}, u32[]{:S(2)}, u32[]{:S(2)}) %collective-permute-start.3) | collective-permute-done | bytes 40992 | tf_op jit(solution)/shard_map/ppermute | solution.py:187
  40.2 0.1 collective-permute-start.4
  40.3 4.0 %collective-permute-done.4 = f32[5,8,256]{2,1,0:T(8,128)S(1)} collective-permute-done((f32[5,8,256]{2,1,0:T(8,128)S(1)}, f32[5,8,256]{2,1,0:T(8,128)S(1)}, u32[]{:S(2)}, u32[]{:S(2)}) %collective-permute-start.4) | collective-permute-done | bytes 40992 | tf_op jit(solution)/shard_map/ppermute | solution.py:187
  44.3 1.3 %collective-permute-start.5 = (f32[5,8,256]{2,1,0:T(8,128)S(1)}, f32[5,8,256]{2,1,0:T(8,128)S(1)}, u32[]{:S(2)}, u32[]{:S(2)}) collective-permute-start(f32[5,8,256]{2,1,0:T(8,128)S(1)} %constant_dynamic-update-slice_fusion.10), channel_id=1, source_target_pairs={{0,16},{2,18},{4,20},{6,22},{8,24},{10,26},{12,28},{14,30},{16,0},... | collective-permute-start | bytes 122888 | tf_op jit(solution)/shard_map/ppermute | solution.py:187
  45.6 3.7 %collective-permute-done.5 = f32[5,8,256]{2,1,0:T(8,128)S(1)} collective-permute-done((f32[5,8,256]{2,1,0:T(8,128)S(1)}, f32[5,8,256]{2,1,0:T(8,128)S(1)}, u32[]{:S(2)}, u32[]{:S(2)}) %collective-permute-start.5) | collective-permute-done | bytes 40992 | tf_op jit(solution)/shard_map/ppermute | solution.py:187
  49.4 0.6 %pad_maximum_fusion.1.ends_ref = f32[2,8,256]{2,1,0:T(8,128)} fusion(f32[1,8,256]{2,1,0:T(8,128)S(1)} %broadcast_select_fusion.14, f32[1,8,256]{2,1,0:T(8,128)S(1)} %get-tuple-element.15), kind=kLoop, calls=%fused_computation.24 | loop fusion | flops 4096 | bytes 32768 | tf_op jit(solution)/shard_map/stack | solution.py:200
  50.0 1.8 %finish.1 = f32[24,8,256]{2,1,0:T(8,128)} custom-call(f32[23,3,8,256]{3,2,1,0:T(8,128)} %get-tuple-element.13.joint_ref, f32[2,8,256]{2,1,0:T(8,128)} %pad_maximum_fusion.1.ends_ref), custom_call_target="tpu_custom_call" | custom-call | tf_op jit(solution)/shard_map/finish/pallas_call | solution.py:201
  (22 shorter events, 0.2 us)
Async XLA Ops:
  0.0 0.7 %slice-start = ((f32[24,8,256]{2,1,0:T(8,128)}), f32[2,8,256]{2,1,0:T(8,128)S(1)}, s32[]{:S(2)}) async-start(f32[24,8,256]{2,1,0:T(8,128)} %c_ref.3), calls=%async_computation | async-start | bytes 32768 | tf_op jit(solution)/shard_map/slice | solution.py:166
  0.0 0.7 %slice-start.1 = ((f32[24,8,256]{2,1,0:T(8,128)}), f32[2,8,256]{2,1,0:T(8,128)S(1)}, s32[]{:S(2)}) async-start(f32[24,8,256]{2,1,0:T(8,128)} %v_ref.1), calls=%async_computation.1 | async-start | bytes 32768 | tf_op jit(solution)/shard_map/slice | solution.py:166
  0.0 0.7 %slice-start.2 = ((f32[24,8,256]{2,1,0:T(8,128)}), f32[1,8,256]{2,1,0:T(8,128)S(1)}, s32[]{:S(2)}) async-start(f32[24,8,256]{2,1,0:T(8,128)} %e_ref.1), calls=%async_computation.2 | async-start | bytes 16384 | tf_op jit(solution)/shard_map/slice | solution.py:166
  0.7 9.0 %collective-permute-start = (f32[5,8,256]{2,1,0:T(8,128)S(1)}, f32[5,8,256]{2,1,0:T(8,128)S(1)}, u32[]{:S(2)}, u32[]{:S(2)}) collective-permute-start(f32[5,8,256]{2,1,0:T(8,128)S(1)} %pad_maximum_fusion), channel_id=1, source_target_pairs={{0,2},{2,4},{4,6},{6,8},{8,10},{10,12},{12,14},{14,16},{16,18},{18... | collective-permute-start | bytes 122888 | tf_op jit(solution)/shard_map/ppermute | solution.py:167
  9.7 0.6 %copy-start = (f32[5,8,256]{2,1,0:T(8,128)}, f32[5,8,256]{2,1,0:T(8,128)S(1)}, u32[]{:S(2)}) copy-start(f32[5,8,256]{2,1,0:T(8,128)S(1)} %collective-permute-done.h_ref) | copy-start | bytes 122884
  26.5 1.5 %collective-permute-start.1 = (f32[24,8,128]{2,1,0:T(8,128)}, f32[24,8,128]{2,1,0:T(8,128)S(1)}, u32[]{:S(2)}, u32[]{:S(2)}) collective-permute-start(f32[24,8,128]{2,1,0:T(8,128)} %get-tuple-element.12.mine_ref), channel_id=1, source_target_pairs={{0,1},{1,0},{2,3},{3,2},{4,5},{5,4},{6,7},{7,6},{8,9},{9,8},{10,11... | collective-permute-start | bytes 294920 | tf_op jit(solution)/shard_map/ppermute | solution.py:174
  28.0 0.6 %copy-start.1 = (f32[24,8,128]{2,1,0:T(8,128)}, f32[24,8,128]{2,1,0:T(8,128)S(1)}, u32[]{:S(2)}) copy-start(f32[24,8,128]{2,1,0:T(8,128)S(1)} %collective-permute-done.1.theirs_ref) | copy-start | bytes 294916
  30.9 4.2 %collective-permute-start.2 = (f32[5,8,256]{2,1,0:T(8,128)}, f32[5,8,256]{2,1,0:T(8,128)S(1)}, u32[]{:S(2)}, u32[]{:S(2)}) collective-permute-start(f32[5,8,256]{2,1,0:T(8,128)} %get-tuple-element.14), channel_id=1, source_target_pairs={{0,2},{2,0},{4,6},{6,4},{8,10},{10,8},{12,14},{14,12},{16,18},{18,... | collective-permute-start | bytes 122888 | tf_op jit(solution)/shard_map/ppermute | solution.py:187
  36.0 4.1 %collective-permute-start.3 = (f32[5,8,256]{2,1,0:T(8,128)S(1)}, f32[5,8,256]{2,1,0:T(8,128)S(1)}, u32[]{:S(2)}, u32[]{:S(2)}) collective-permute-start(f32[5,8,256]{2,1,0:T(8,128)S(1)} %constant_dynamic-update-slice_fusion), channel_id=1, source_target_pairs={{0,4},{2,6},{4,0},{6,2},{8,12},{10,14},{12,8},{14,10},{16,20},{18,... | collective-permute-start | bytes 122888 | tf_op jit(solution)/shard_map/ppermute | solution.py:187
  40.2 4.1 %collective-permute-start.4 = (f32[5,8,256]{2,1,0:T(8,128)S(1)}, f32[5,8,256]{2,1,0:T(8,128)S(1)}, u32[]{:S(2)}, u32[]{:S(2)}) collective-permute-start(f32[5,8,256]{2,1,0:T(8,128)S(1)} %constant_dynamic-update-slice_fusion.5), channel_id=1, source_target_pairs={{0,8},{2,10},{4,12},{6,14},{8,0},{10,2},{12,4},{14,6},{16,24},{18,... | collective-permute-start | bytes 122888 | tf_op jit(solution)/shard_map/ppermute | solution.py:187
  44.3 5.0 %collective-permute-start.5 = (f32[5,8,256]{2,1,0:T(8,128)S(1)}, f32[5,8,256]{2,1,0:T(8,128)S(1)}, u32[]{:S(2)}, u32[]{:S(2)}) collective-permute-start(f32[5,8,256]{2,1,0:T(8,128)S(1)} %constant_dynamic-update-slice_fusion.10), channel_id=1, source_target_pairs={{0,16},{2,18},{4,20},{6,22},{8,24},{10,26},{12,28},{14,30},{16,0},... | collective-permute-start | bytes 122888 | tf_op jit(solution)/shard_map/ppermute | solution.py:187
where the time goes:
time: 52.1 us; the launch traced here: 51.8 us
  waiting for transfers between devices  23.4 us (45%)
  Pallas kernels  20.3 us (39%)
  starting transfers between devices  4.4 us (8%)
  local copies, waits for them, and re-layouts  1.98 us (4%)
  other arithmetic  1.61 us (3%)
    pallas_call x1, Pallas kernels, per_device(): pl.pallas_call(wall_kernel, out_shape=[shape, shape, jax.ShapeDtypeStruct...  16.2 us
    ppermute x4, waiting for transfers between devices, per_device(): partner = lax.ppermute(block, 'gx', [(i, i ^ bit) for i in range(count)])  15.9 us
    ppermute x1, waiting for transfers between devices, per_device(): lax.ppermute(tail, 'gx', [(i, (i + 1) % count) for i in range(count)])  5.97 us
    ppermute x1, starting transfers between devices, per_device(): lax.ppermute(tail, 'gx', [(i, (i + 1) % count) for i in range(count)])  2.98 us
    pallas_call x1, Pallas kernels, per_device(): pl.pallas_call(reduce_kernel, out_shape=[jax.ShapeDtypeStruct((5, planes,...  2.31 us
    pallas_call x1, Pallas kernels, per_device(): pl.pallas_call(finish_kernel, out_shape=shape, name='finish')(joints, ends)  1.77 us
    ppermute x1, waiting for transfers between devices, per_device(): other = lax.ppermute(edge, 'gy', [(0, 1), (1, 0)])  1.51 us
    ppermute x4, starting transfers between devices, per_device(): partner = lax.ppermute(block, 'gx', [(i, i ^ bit) for i in range(count)])  1.42 us
  transfers between devices with their start and end apart: 6, of which 6 were waited for; matrix products, arithmetic and copies ran while one was open for 0% of the time, Pallas kernels for 0%

commit v1 on v0

v1 whole, which is shorter than its diff:
```python
import jax
import jax.numpy as jnp
from jax import lax
from jax.experimental import pallas as pl
from jax.experimental.pallas import tpu as pltpu
from jax.sharding import PartitionSpec as P

stream_rate = 1000.0
normal_rate = 50.0


def merge(a, b):
    oa, sla, sra, rla, rra = a
    ob, slb, srb, rlb, rrb = b
    sm = slb if sra is None else sra + slb
    rm = rlb if rra is None else rra + rlb
    t = 1.0 / (oa + ob + sm)
    ga = oa * t
    gb = ob * t
    gsb = gb * sm
    grb = gb * rm
    block = (
        oa * gb,
        sla + ga * sm,
        gsb if srb is None else srb + gsb,
        rla + ga * rm,
        grb if rrb is None else rrb + grb,
    )
    return block, (t * rm, ga, gb)


def tree_up(lo, hi, leaf, keep):
    if hi - lo == 1:
        return leaf(lo)
    mid = (lo + hi) // 2
    block, joint = merge(tree_up(lo, mid, leaf, keep), tree_up(mid, hi, leaf, keep))
    keep(mid, joint)
    return block


def tree_down(lo, hi, left, right, joint, put):
    if hi - lo == 1:
        return
    mid = (lo + hi) // 2
    z, ga, gb = joint(mid)
    value = z + ga * left + gb * right
    put(mid, value)
    tree_down(lo, mid, left, value, joint, put)
    tree_down(mid, hi, value, right, joint, put)


def wall_kernel(v_ref, c_ref, e_ref, h_ref, lap_ref, joint_ref, edge_ref, far_ref, rs, cs):
    rows, planes, width = v_ref.shape
    lines = rows * planes
    seg = width // 8
    upper = lax.axis_index("gy") == 1
    lower = jnp.logical_not(upper)

    def vel(i):
        return h_ref[i + 2] if i < 0 else v_ref[i]

    def visc(i):
        return h_ref[i + 4] if i < 0 else c_ref[i]

    def expl(i):
        return h_ref[4] if i < 0 else e_ref[i]

    right_sides, coefs = [], []
    flux = 0.5 * stream_rate * (visc(-1) + visc(-2)) * (vel(-1) - vel(-2))
    for i in range(-1, rows - 1):
        v = vel(i)
        c = visc(i)
        east = 0.5 * stream_rate * (c + visc(i + 1)) * (vel(i + 1) - v)
        lap = east - flux
        flux = east
        lap_ref[i + 1] = lap
        right_sides.append(v + lap + expl(i))
        coefs.append(c)
    spare = -lines % 128 // planes
    turn(right_sides + right_sides[:spare], rs)
    turn(coefs + coefs[:spare], cs)

    def load(ref, m):
        return jnp.concatenate(
            [ref[n, pl.ds(m, 8, stride=seg), :] for n in range(ref.shape[0])], axis=1
        )

    sub = lax.broadcasted_iota(jnp.int32, (8, rs.shape[0] * 128), 0)
    one = jnp.ones(sub.shape, jnp.float32)
    c_first = load(cs, 0)
    c_last = load(cs, seg - 1)
    s_first = one + jnp.where((sub == 0) & lower, normal_rate * c_first, 0.0)
    s_last = one + jnp.where((sub == 7) & upper, normal_rate * c_last, 0.0)

    def leaf(m):
        o = 0.5 * normal_rate * (load(cs, m) + load(cs, m + 1))
        s = s_first if m == 0 else one
        if m == seg - 2:
            return (o, s, s_last, load(rs, m), load(rs, m + 1))
        return (o, s, None, load(rs, m), None)

    def keep(m, joint):
        for n in range(3):
            joint_ref[m - 1, n] = joint[n]

    block = tree_up(0, seg - 1, leaf, keep)
    link = 0.5 * normal_rate * (c_last + pltpu.roll(c_first, 7, 0))
    zero = jnp.zeros_like(one)
    linked, joint = merge(block, (link, zero, None, zero, None))
    last = sub == 7
    block = tuple(jnp.where(last, x, y) for x, y in zip(block, linked))
    keep(seg - 1, tuple(jnp.where(last, x, y) for x, y in zip((zero, zero, one), joint)))
    for n, h in enumerate((1, 2, 4)):
        block, joint = merge(block, tuple(pltpu.roll(x, 8 - h, 0) for x in block))
        keep(seg + n, joint)
    o, sl, sr, rl, rr = block
    s_far = jnp.where(upper, sr, sl)
    s_near = jnp.where(upper, sl, sr)
    r_far = jnp.where(upper, rr, rl)
    r_near = jnp.where(upper, rl, rr)
    t = 1.0 / (o + s_far)
    c_edge = jnp.where(upper, c_first, pltpu.roll(c_last, 1, 0))
    ot = o * t
    edge_ref[...] = jnp.where(
        sub == 0,
        s_near + ot * s_far,
        jnp.where(sub == 1, pltpu.roll(r_near + ot * r_far, 1, 0), pltpu.roll(c_edge, 2, 0)),
    )
    far_ref[0] = t * r_far
    far_ref[1] = ot


def turn(blocks, ref):
    per = 128 // blocks[0].shape[0]
    for n in range(ref.shape[0]):
        ref[n] = jnp.concatenate(blocks[n * per : (n + 1) * per], axis=0).T


def reduce_kernel(
    c_ref, h_ref, lap_ref, wall_ref, far_ref, mine_ref, theirs_ref, block_ref, joint_ref, ps
):
    rows, planes, width = c_ref.shape
    seg = width // 8
    upper = lax.axis_index("gy") == 1
    s0, r0, c0 = (mine_ref[n : n + 1] for n in range(3))
    s1, r1, c1 = (theirs_ref[n : n + 1] for n in range(3))
    face = 0.5 * normal_rate * (c0 + c1)
    ft = face / (s1 + face)
    near = (r0 + ft * r1) / (s0 + ft * s1)
    near = jnp.broadcast_to(near, mine_ref.shape)
    far = far_ref[0] + far_ref[1] * near
    left = jnp.where(upper, near, far)
    right = jnp.where(upper, far, near)
    sub = lax.broadcasted_iota(jnp.int32, left.shape, 0)

    def wall_joint(m):
        return tuple(wall_ref[m - 1, n] for n in range(3))

    for n, h in ((2, 4), (1, 2), (0, 1)):
        z, ga, gb = wall_joint(seg + n)
        mid = z + ga * left + gb * right
        fresh = (sub & h) != 0
        left, right = (
            jnp.where(fresh, pltpu.roll(mid, h, 0), left),
            jnp.where(fresh, pltpu.roll(right, h, 0), mid),
        )

    def put(m, value):
        for n in range(ps.shape[0]):
            ps[n, pl.ds(m, 8, stride=seg), :] = value[:, n * 128 : (n + 1) * 128]

    put(0, left)
    z, ga, gb = wall_joint(seg - 1)
    end = z + ga * left + gb * right
    put(seg - 1, end)
    tree_down(0, seg - 1, left, end, wall_joint, put)
    turned = [ps[n].T for n in range(ps.shape[0])]
    per = 128 // planes

    def visc(i):
        return h_ref[i + 4] if i < 0 else c_ref[i]

    def leaf(r):
        at = r % per * planes
        q = turned[r // per][at : at + planes] - lap_ref[r]
        o = 0.5 * stream_rate * (visc(r - 1) + visc(r))
        return (o, jnp.ones_like(q), None, q, None)

    def keep(m, joint):
        for n in range(3):
            joint_ref[m - 1, n] = joint[n]

    whole = tree_up(0, rows, leaf, keep)
    for n in range(5):
        block_ref[n] = whole[n]


def finish_kernel(joint_ref, ends_ref, out_ref):
    rows = out_ref.shape[0]

    def joint(m):
        return tuple(joint_ref[m - 1, n] for n in range(3))

    def put(m, value):
        out_ref[m - 1] = value

    put(rows, ends_ref[1])
    tree_down(0, rows, ends_ref[0], ends_ref[1], joint, put)


def per_device(velocity, viscosity, explicit):
    rows, planes, width = velocity.shape
    f32 = jnp.float32
    count = lax.axis_size("gx")
    tail = jnp.concatenate([velocity[-2:], viscosity[-2:], explicit[-1:]], axis=0)
    halo = lax.ppermute(tail, "gx", [(i, (i + 1) % count) for i in range(count)])
    shape = jax.ShapeDtypeStruct((rows, planes, width), f32)
    tiles = -(-rows * planes // 128)
    seg = width // 8
    lap, wall, edge, far = pl.pallas_call(
        wall_kernel,
        out_shape=[
            shape,
            jax.ShapeDtypeStruct((seg + 2, 3, 8, tiles * 128), f32),
            jax.ShapeDtypeStruct((8, tiles * 128), f32),
            jax.ShapeDtypeStruct((2, 8, tiles * 128), f32),
        ],
        scratch_shapes=[pltpu.VMEM((tiles, width, 128), f32)] * 2,
        name="wall",
    )(velocity, viscosity, explicit, halo)
    other = lax.ppermute(edge, "gy", [(0, 1), (1, 0)])
    block, joints = pl.pallas_call(
        reduce_kernel,
        out_shape=[
            jax.ShapeDtypeStruct((5, planes, width), f32),
            jax.ShapeDtypeStruct((rows - 1, 3, planes, width), f32),
        ],
        scratch_shapes=[pltpu.VMEM((tiles, width, 128), f32)],
        name="reduce",
    )(viscosity, halo, lap, wall, far, edge, other)
    rank = lax.axis_index("gx")
    path = []
    bit = 1
    while bit < count:
        partner = lax.ppermute(block, "gx", [(i, i ^ bit) for i in range(count)])
        right = (rank & bit) != 0
        a = jnp.where(right, partner, block)
        b = jnp.where(right, block, partner)
        whole, joint = merge(tuple(a[n] for n in range(5)), tuple(b[n] for n in range(5)))
        path.append((right, joint))
        block = jnp.stack(whole)
        bit *= 2
    top = (block[3] + block[4]) / (block[1] + block[2])
    low, high = top, top
    for right, (z, ga, gb) in reversed(path):
        mid = z + ga * low + gb * high
        low, high = jnp.where(right, mid, low), jnp.where(right, high, mid)
    ends = jnp.stack([low, high])
    return pl.pallas_call(finish_kernel, out_shape=shape, name="finish")(joints, ends)


def solution(mesh):
    return jax.shard_map(
        per_device,
        mesh=mesh,
        in_specs=(P("gx", None, "gy"), P("gx", None, "gy"), P("gx", None, "gy")),
        out_specs=P("gx", None, "gy"),
        check_vma=False,
    )
```

time: 52.1 us -> 38.6 us (0.74)
  Pallas kernels: 20.3 us -> 6.93 us
    pallas_call x1, Pallas kernels: 16.2 us -> 2.69 us  [per_device(): pl.pallas_call(wall_kernel, out_shape=[shape, jax.ShapeDtypeStruct((seg +...]
where the time goes in v1:
time: 38.6 us; the launch traced here: 38.3 us
  waiting for transfers between devices  23.2 us (60%)
  Pallas kernels  6.93 us (18%)
  starting transfers between devices  4.39 us (11%)
  local copies, waits for them, and re-layouts  1.94 us (5%)
  other arithmetic  1.61 us (4%)
    ppermute x4, waiting for transfers between devices, per_device(): partner = lax.ppermute(block, 'gx', [(i, i ^ bit) for i in range(count)])  15.9 us
    ppermute x1, waiting for transfers between devices, per_device(): lax.ppermute(tail, 'gx', [(i, (i + 1) % count) for i in range(count)])  5.97 us
    ppermute x1, starting transfers between devices, per_device(): lax.ppermute(tail, 'gx', [(i, (i + 1) % count) for i in range(count)])  2.98 us
    pallas_call x1, Pallas kernels, per_device(): pl.pallas_call(wall_kernel, out_shape=[shape, jax.ShapeDtypeStruct((seg +...  2.69 us
    pallas_call x1, Pallas kernels, per_device(): pl.pallas_call(reduce_kernel, out_shape=[jax.ShapeDtypeStruct((5, planes,...  2.47 us
    pallas_call x1, Pallas kernels, per_device(): pl.pallas_call(finish_kernel, out_shape=shape, name='finish')(joints, ends)  1.77 us
    ppermute x4, starting transfers between devices, per_device(): partner = lax.ppermute(block, 'gx', [(i, i ^ bit) for i in range(count)])  1.41 us
    ppermute x1, waiting for transfers between devices, per_device(): other = lax.ppermute(edge, 'gy', [(0, 1), (1, 0)])  1.38 us
  transfers between devices with their start and end apart: 6, of which 6 were waited for; matrix products, arithmetic and copies ran while one was open for 0% of the time, Pallas kernels for 0%

profile of v1, /device:TPU:0, one launch (start us, length us, event | category | flops | bytes accessed | tf_op | source)
XLA Modules:
  0.0 38.3 jit_solution(4565778766360080790)
XLA Ops:
  0.0 0.0 slice-start
  0.0 0.0 slice-start.1
  0.0 0.0 slice-start.2
  0.0 0.7 %slice-done = f32[2,8,256]{2,1,0:T(8,128)S(1)} async-done(((f32[24,8,256]{2,1,0:T(8,128)}), f32[2,8,256]{2,1,0:T(8,128)S(1)}, s32[]{:S(2)}) %slice-start) | async-done | bytes 16408 | tf_op jit(solution)/shard_map/slice | solution.py:215
  0.7 0.0 slice-done.1
  0.7 0.0 slice-done.2
  0.7 3.0 %collective-permute-start = (f32[5,8,256]{2,1,0:T(8,128)S(1)}, f32[5,8,256]{2,1,0:T(8,128)S(1)}, u32[]{:S(2)}, u32[]{:S(2)}) collective-permute-start(f32[5,8,256]{2,1,0:T(8,128)S(1)} %pad_maximum_fusion), channel_id=1, source_target_pairs={{0,2},{2,4},{4,6},{6,8},{8,10},{10,12},{12,14},{14,16},{16,18},{18... | collective-permute-start | bytes 122888 | tf_op jit(solution)/shard_map/ppermute | solution.py:216
  3.7 6.0 %collective-permute-done.h_ref = f32[5,8,256]{2,1,0:T(8,128)S(1)} collective-permute-done((f32[5,8,256]{2,1,0:T(8,128)S(1)}, f32[5,8,256]{2,1,0:T(8,128)S(1)}, u32[]{:S(2)}, u32[]{:S(2)}) %collective-permute-start) | collective-permute-done | bytes 40992 | tf_op jit(solution)/shard_map/ppermute | solution.py:216
  9.7 0.0 copy-start
  9.7 0.6 %copy-done = f32[5,8,256]{2,1,0:T(8,128)} copy-done((f32[5,8,256]{2,1,0:T(8,128)}, f32[5,8,256]{2,1,0:T(8,128)S(1)}, u32[]{:S(2)}) %copy-start) | copy-done | bytes 40984
  10.3 2.7 %wall.1 = (f32[24,8,256]{2,1,0:T(8,128)}, f32[34,3,8,256]{3,2,1,0:T(8,128)}, f32[8,256]{1,0:T(8,128)}, f32[2,8,256]{2,1,0:T(8,128)}) custom-call(f32[24,8,256]{2,1,0:T(8,128)} %v_ref.1, f32[24,8,256]{2,1,0:T(8,128)} %c_ref.3, f32[24,8,256]{2,1,0:T(8,128)} %e_ref.1, f32[5,8,256]{2,1,0:T(8,128)} %copy-done), custom_call_target="tpu_custom_call" | custom-call | tf_op jit(solution)/shard_map/wall/pallas_call | solution.py:220
  13.0 0.0 collective-permute-start.1
  13.0 1.4 %collective-permute-done.1.theirs_ref = f32[8,256]{1,0:T(8,128)S(1)} collective-permute-done((f32[8,256]{1,0:T(8,128)}, f32[8,256]{1,0:T(8,128)S(1)}, u32[]{:S(2)}, u32[]{:S(2)}) %collective-permute-start.1) | collective-permute-done | bytes 8224 | tf_op jit(solution)/shard_map/ppermute | solution.py:231
  14.4 0.0 copy-start.1
  14.4 0.6 %copy-done.1 = f32[8,256]{1,0:T(8,128)} copy-done((f32[8,256]{1,0:T(8,128)}, f32[8,256]{1,0:T(8,128)S(1)}, u32[]{:S(2)}) %copy-start.1) | copy-done | bytes 8216
  15.0 2.5 %reduce.1 = (f32[5,8,256]{2,1,0:T(8,128)}, f32[23,3,8,256]{3,2,1,0:T(8,128)}) custom-call(f32[24,8,256]{2,1,0:T(8,128)} %c_ref.3, f32[5,8,256]{2,1,0:T(8,128)} %copy-done, f32[24,8,256]{2,1,0:T(8,128)} %get-tuple-element.11.lap_ref, f32[34,3,8,256]{3,2,1,0:T(8,128)} %get-tuple-element.12.wall_ref, f32[2,8,256]{2,1,0:T(8,128)} %get-tuple-element.13.far_ref, ...), custom_call_target="tpu_custom_call" | custom-call | tf_op jit(solution)/shard_map/reduce/pallas_call | solution.py:232
  17.5 0.0 collective-permute-start.2
  17.5 4.2 %collective-permute-done.2 = f32[5,8,256]{2,1,0:T(8,128)S(1)} collective-permute-done((f32[5,8,256]{2,1,0:T(8,128)}, f32[5,8,256]{2,1,0:T(8,128)S(1)}, u32[]{:S(2)}, u32[]{:S(2)}) %collective-permute-start.2) | collective-permute-done | bytes 40992 | tf_op jit(solution)/shard_map/ppermute | solution.py:245
  21.7 0.8 %broadcast_select_fusion.6 = (f32[5,8,256]{2,1,0:T(8,128)S(1)}, f32[5,8,256]{2,1,0:T(8,128)S(1)}) fusion(f32[5,8,256]{2,1,0:T(8,128)} %get-tuple-element.16, f32[5,8,256]{2,1,0:T(8,128)S(1)} %collective-permute-done.2, pred[]{:T(512)S(6)} %ne.12), kind=kLoop, calls=%fused_computation.22 | loop fusion | flops 20480 | bytes 163841 | tf_op jit(solution)/shard_map/jit(_where)/select_n | solution.py:248
  22.5 0.1 collective-permute-start.3
  22.6 4.0 %collective-permute-done.3 = f32[5,8,256]{2,1,0:T(8,128)S(1)} collective-permute-done((f32[5,8,256]{2,1,0:T(8,128)S(1)}, f32[5,8,256]{2,1,0:T(8,128)S(1)}, u32[]{:S(2)}, u32[]{:S(2)}) %collective-permute-start.3) | collective-permute-done | bytes 40992 | tf_op jit(solution)/shard_map/ppermute | solution.py:245
  26.7 0.1 collective-permute-start.4
  26.8 4.0 %collective-permute-done.4 = f32[5,8,256]{2,1,0:T(8,128)S(1)} collective-permute-done((f32[5,8,256]{2,1,0:T(8,128)S(1)}, f32[5,8,256]{2,1,0:T(8,128)S(1)}, u32[]{:S(2)}, u32[]{:S(2)}) %collective-permute-start.4) | collective-permute-done | bytes 40992 | tf_op jit(solution)/shard_map/ppermute | solution.py:245
  30.8 1.3 %collective-permute-start.5 = (f32[5,8,256]{2,1,0:T(8,128)S(1)}, f32[5,8,256]{2,1,0:T(8,128)S(1)}, u32[]{:S(2)}, u32[]{:S(2)}) collective-permute-start(f32[5,8,256]{2,1,0:T(8,128)S(1)} %constant_dynamic-update-slice_fusion.10), channel_id=1, source_target_pairs={{0,16},{2,18},{4,20},{6,22},{8,24},{10,26},{12,28},{14,30},{16,0},... | collective-permute-start | bytes 122888 | tf_op jit(solution)/shard_map/ppermute | solution.py:245
  32.1 3.7 %collective-permute-done.5 = f32[5,8,256]{2,1,0:T(8,128)S(1)} collective-permute-done((f32[5,8,256]{2,1,0:T(8,128)S(1)}, f32[5,8,256]{2,1,0:T(8,128)S(1)}, u32[]{:S(2)}, u32[]{:S(2)}) %collective-permute-start.5) | collective-permute-done | bytes 40992 | tf_op jit(solution)/shard_map/ppermute | solution.py:245
  35.9 0.6 %pad_maximum_fusion.1.ends_ref = f32[2,8,256]{2,1,0:T(8,128)} fusion(f32[1,8,256]{2,1,0:T(8,128)S(1)} %broadcast_select_fusion.14, f32[1,8,256]{2,1,0:T(8,128)S(1)} %get-tuple-element.17), kind=kLoop, calls=%fused_computation.24 | loop fusion | flops 4096 | bytes 32768 | tf_op jit(solution)/shard_map/stack | solution.py:258
  36.5 1.8 %finish.1 = f32[24,8,256]{2,1,0:T(8,128)} custom-call(f32[23,3,8,256]{3,2,1,0:T(8,128)} %get-tuple-element.15.joint_ref, f32[2,8,256]{2,1,0:T(8,128)} %pad_maximum_fusion.1.ends_ref), custom_call_target="tpu_custom_call" | custom-call | tf_op jit(solution)/shard_map/finish/pallas_call | solution.py:259
  (22 shorter events, 0.2 us)
Async XLA Ops:
  0.0 0.7 %slice-start = ((f32[24,8,256]{2,1,0:T(8,128)}), f32[2,8,256]{2,1,0:T(8,128)S(1)}, s32[]{:S(2)}) async-start(f32[24,8,256]{2,1,0:T(8,128)} %c_ref.3), calls=%async_computation | async-start | bytes 32768 | tf_op jit(solution)/shard_map/slice | solution.py:215
  0.0 0.7 %slice-start.1 = ((f32[24,8,256]{2,1,0:T(8,128)}), f32[2,8,256]{2,1,0:T(8,128)S(1)}, s32[]{:S(2)}) async-start(f32[24,8,256]{2,1,0:T(8,128)} %v_ref.1), calls=%async_computation.1 | async-start | bytes 32768 | tf_op jit(solution)/shard_map/slice | solution.py:215
  0.0 0.7 %slice-start.2 = ((f32[24,8,256]{2,1,0:T(8,128)}), f32[1,8,256]{2,1,0:T(8,128)S(1)}, s32[]{:S(2)}) async-start(f32[24,8,256]{2,1,0:T(8,128)} %e_ref.1), calls=%async_computation.2 | async-start | bytes 16384 | tf_op jit(solution)/shard_map/slice | solution.py:215
  0.7 9.0 %collective-permute-start = (f32[5,8,256]{2,1,0:T(8,128)S(1)}, f32[5,8,256]{2,1,0:T(8,128)S(1)}, u32[]{:S(2)}, u32[]{:S(2)}) collective-permute-start(f32[5,8,256]{2,1,0:T(8,128)S(1)} %pad_maximum_fusion), channel_id=1, source_target_pairs={{0,2},{2,4},{4,6},{6,8},{8,10},{10,12},{12,14},{14,16},{16,18},{18... | collective-permute-start | bytes 122888 | tf_op jit(solution)/shard_map/ppermute | solution.py:216
  9.7 0.6 %copy-start = (f32[5,8,256]{2,1,0:T(8,128)}, f32[5,8,256]{2,1,0:T(8,128)S(1)}, u32[]{:S(2)}) copy-start(f32[5,8,256]{2,1,0:T(8,128)S(1)} %collective-permute-done.h_ref) | copy-start | bytes 122884
  13.0 1.4 %collective-permute-start.1 = (f32[8,256]{1,0:T(8,128)}, f32[8,256]{1,0:T(8,128)S(1)}, u32[]{:S(2)}, u32[]{:S(2)}) collective-permute-start(f32[8,256]{1,0:T(8,128)} %get-tuple-element.14.mine_ref), channel_id=1, source_target_pairs={{0,1},{1,0},{2,3},{3,2},{4,5},{5,4},{6,7},{7,6},{8,9},{9,8},{10,11... | collective-permute-start | bytes 24584 | tf_op jit(solution)/shard_map/ppermute | solution.py:231
  14.4 0.6 %copy-start.1 = (f32[8,256]{1,0:T(8,128)}, f32[8,256]{1,0:T(8,128)S(1)}, u32[]{:S(2)}) copy-start(f32[8,256]{1,0:T(8,128)S(1)} %collective-permute-done.1.theirs_ref) | copy-start | bytes 24580
  17.5 4.2 %collective-permute-start.2 = (f32[5,8,256]{2,1,0:T(8,128)}, f32[5,8,256]{2,1,0:T(8,128)S(1)}, u32[]{:S(2)}, u32[]{:S(2)}) collective-permute-start(f32[5,8,256]{2,1,0:T(8,128)} %get-tuple-element.16), channel_id=1, source_target_pairs={{0,2},{2,0},{4,6},{6,4},{8,10},{10,8},{12,14},{14,12},{16,18},{18,... | collective-permute-start | bytes 122888 | tf_op jit(solution)/shard_map/ppermute | solution.py:245
  22.5 4.1 %collective-permute-start.3 = (f32[5,8,256]{2,1,0:T(8,128)S(1)}, f32[5,8,256]{2,1,0:T(8,128)S(1)}, u32[]{:S(2)}, u32[]{:S(2)}) collective-permute-start(f32[5,8,256]{2,1,0:T(8,128)S(1)} %constant_dynamic-update-slice_fusion), channel_id=1, source_target_pairs={{0,4},{2,6},{4,0},{6,2},{8,12},{10,14},{12,8},{14,10},{16,20},{18,... | collective-permute-start | bytes 122888 | tf_op jit(solution)/shard_map/ppermute | solution.py:245
  26.7 4.1 %collective-permute-start.4 = (f32[5,8,256]{2,1,0:T(8,128)S(1)}, f32[5,8,256]{2,1,0:T(8,128)S(1)}, u32[]{:S(2)}, u32[]{:S(2)}) collective-permute-start(f32[5,8,256]{2,1,0:T(8,128)S(1)} %constant_dynamic-update-slice_fusion.5), channel_id=1, source_target_pairs={{0,8},{2,10},{4,12},{6,14},{8,0},{10,2},{12,4},{14,6},{16,24},{18,... | collective-permute-start | bytes 122888 | tf_op jit(solution)/shard_map/ppermute | solution.py:245
  30.8 5.0 %collective-permute-start.5 = (f32[5,8,256]{2,1,0:T(8,128)S(1)}, f32[5,8,256]{2,1,0:T(8,128)S(1)}, u32[]{:S(2)}, u32[]{:S(2)}) collective-permute-start(f32[5,8,256]{2,1,0:T(8,128)S(1)} %constant_dynamic-update-slice_fusion.10), channel_id=1, source_target_pairs={{0,16},{2,18},{4,20},{6,22},{8,24},{10,26},{12,28},{14,30},{16,0},... | collective-permute-start | bytes 122888 | tf_op jit(solution)/shard_map/ppermute | solution.py:245

commit v2 on v1

--- a/solution.py
+++ b/solution.py
@@ -47,6 +47,12 @@
     put(mid, value)
     tree_down(lo, mid, left, value, joint, put)
     tree_down(mid, hi, value, right, joint, put)
+
+
+def load_kernel(v_ref, c_ref, e_ref, v_out, c_out, e_out):
+    v_out[...] = v_ref[...]
+    c_out[...] = c_ref[...]
+    e_out[...] = e_ref[...]
 
 
 def wall_kernel(v_ref, c_ref, e_ref, h_ref, lap_ref, joint_ref, edge_ref, far_ref, rs, cs):
@@ -215,6 +221,13 @@
     tail = jnp.concatenate([velocity[-2:], viscosity[-2:], explicit[-1:]], axis=0)
     halo = lax.ppermute(tail, "gx", [(i, (i + 1) % count) for i in range(count)])
     shape = jax.ShapeDtypeStruct((rows, planes, width), f32)
+    velocity, viscosity, explicit = pl.pallas_call(
+        load_kernel,
+        out_shape=[shape] * 3,
+        cost_estimate=pl.CostEstimate(flops=0, bytes_accessed=8 << 20, transcendentals=0),
+        compiler_params=pltpu.CompilerParams(vmem_limit_bytes=8 << 20),
+        name="load",
+    )(velocity, viscosity, explicit)
     tiles = -(-rows * planes // 128)
     seg = width // 8
     lap, wall, edge, far = pl.pallas_call(
@@ -226,6 +239,7 @@
             jax.ShapeDtypeStruct((2, 8, tiles * 128), f32),
         ],
         scratch_shapes=[pltpu.VMEM((tiles, width, 128), f32)] * 2,
+        compiler_params=pltpu.CompilerParams(vmem_limit_bytes=8 << 20),
         name="wall",
     )(velocity, viscosity, explicit, halo)
     other = lax.ppermute(edge, "gy", [(0, 1), (1, 0)])
@@ -236,6 +250,7 @@
             jax.ShapeDtypeStruct((rows - 1, 3, planes, width), f32),
         ],
         scratch_shapes=[pltpu.VMEM((tiles, width, 128), f32)],
+        compiler_params=pltpu.CompilerParams(vmem_limit_bytes=8 << 20),
         name="reduce",
     )(viscosity, halo, lap, wall, far, edge, other)
     rank = lax.axis_index("gx")
@@ -256,7 +271,12 @@
         mid = z + ga * low + gb * high
         low, high = jnp.where(right, mid, low), jnp.where(right, high, mid)
     ends = jnp.stack([low, high])
-    return pl.pallas_call(finish_kernel, out_shape=shape, name="finish")(joints, ends)
+    return pl.pallas_call(
+        finish_kernel,
+        out_shape=shape,
+        compiler_params=pltpu.CompilerParams(vmem_limit_bytes=8 << 20),
+        name="finish",
+    )(joints, ends)
 
 
 def solution(mesh):

time: 38.6 us -> 30.5 us (0.79)
  Pallas kernels: 6.93 us -> 1.8 us
  waiting for transfers between devices: 23.2 us -> 20 us
  local copies, waits for them, and re-layouts: 1.94 us -> 3.51 us
  other arithmetic: 1.61 us -> 0.24 us
    ppermute x1, waiting for transfers between devices: 5.97 us -> 3.15 us  [per_device(): lax.ppermute(tail, 'gx', [(i, (i + 1) % count) for i in range(count)])]
    pallas_call x1, Pallas kernels: 2.47 us -> 0.34 us  [per_device(): pl.pallas_call(reduce_kernel, out_shape=[jax.ShapeDtypeStruct((5, planes,...]
    pallas_call x1, Pallas kernels: 2.69 us -> 0.7 us  [per_device(): pl.pallas_call(wall_kernel, out_shape=[shape, jax.ShapeDtypeStruct((seg +...]
    unnamed x4 -> x6, local copies, waits for them, and re-layouts: 1.21 us -> 2.78 us
    pallas_call x1 -> x2, Pallas kernels: 1.77 us -> 0.75 us  [the longest x1 0.71 us: per_device(): pl.pallas_call(finish_kernel, out_shape=shape, compiler_params=pltpu.Comp...]
    select_n x3, other arithmetic: 0.8 us -> 0.03 us  [per_device(): b = jnp.where(right, block, partner)]
    slice x2, local copies, waits for them, and re-layouts: 0.02 us -> 0.71 us  [per_device(): velocity[-2:]]
    slice x2, local copies, waits for them, and re-layouts: 0.71 us -> 0.02 us  [per_device(): viscosity[-2:]]
where the time goes in v2:
time: 30.5 us; the launch traced here: 30.2 us
  waiting for transfers between devices  20 us (66%)
  starting transfers between devices  4.53 us (15%)
  local copies, waits for them, and re-layouts  3.51 us (12%)
  Pallas kernels  1.8 us (6%)
    ppermute x4, waiting for transfers between devices, per_device(): partner = lax.ppermute(block, 'gx', [(i, i ^ bit) for i in range(count)])  15.7 us
    ppermute x1, waiting for transfers between devices, per_device(): lax.ppermute(tail, 'gx', [(i, (i + 1) % count) for i in range(count)])  3.15 us
    ppermute x1, starting transfers between devices, per_device(): lax.ppermute(tail, 'gx', [(i, (i + 1) % count) for i in range(count)])  2.98 us
    unnamed x6, local copies, waits for them, and re-layouts  2.78 us
    ppermute x4, starting transfers between devices, per_device(): partner = lax.ppermute(block, 'gx', [(i, i ^ bit) for i in range(count)])  1.48 us
    ppermute x1, waiting for transfers between devices, per_device(): other = lax.ppermute(edge, 'gy', [(0, 1), (1, 0)])  1.16 us
    slice x2, local copies, waits for them, and re-layouts, per_device(): velocity[-2:]  0.71 us
    pallas_call x1, Pallas kernels, per_device(): pl.pallas_call(finish_kernel, out_shape=shape, compiler_params=pltpu.Comp...  0.71 us
  transfers between devices with their start and end apart: 6, of which 6 were waited for; matrix products, arithmetic and copies ran while one was open for 0% of the time, Pallas kernels for 0%

profile of v2, /device:TPU:0, one launch (start us, length us, event | category | flops | bytes accessed | tf_op | source)
XLA Modules:
  0.0 30.2 jit_solution(7547477883033466720)
XLA Ops:
  0.0 0.0 slice-start
  0.0 0.0 slice-start.1
  0.0 0.0 slice-start.2
  0.0 0.7 %slice-done = f32[2,8,256]{2,1,0:T(8,128)S(1)} async-done(((f32[24,8,256]{2,1,0:T(8,128)}), f32[2,8,256]{2,1,0:T(8,128)S(1)}, s32[]{:S(2)}) %slice-start) | async-done | bytes 16408 | tf_op jit(solution)/shard_map/slice | solution.py:221
  0.7 0.0 slice-done.1
  0.7 0.0 slice-done.2
  0.7 3.0 %collective-permute-start = (f32[5,8,256]{2,1,0:T(8,128)S(1)}, f32[5,8,256]{2,1,0:T(8,128)S(1)}, u32[]{:S(2)}, u32[]{:S(2)}) collective-permute-start(f32[5,8,256]{2,1,0:T(8,128)S(1)} %pad_maximum_fusion), channel_id=1, source_target_pairs={{0,2},{2,4},{4,6},{6,8},{8,10},{10,12},{12,14},{14,16},{16,18},{18... | collective-permute-start | bytes 122888 | tf_op jit(solution)/shard_map/ppermute | solution.py:222
  3.7 0.0 copy-start
  3.7 0.9 %copy-done = f32[24,8,256]{2,1,0:T(8,128)S(1)} copy-done((f32[24,8,256]{2,1,0:T(8,128)S(1)}, f32[24,8,256]{2,1,0:T(8,128)}, u32[]{:S(2)}) %copy-start) | copy-done | bytes 196632
  4.7 0.0 copy-start.1
  4.7 0.9 %copy-done.1 = f32[24,8,256]{2,1,0:T(8,128)S(1)} copy-done((f32[24,8,256]{2,1,0:T(8,128)S(1)}, f32[24,8,256]{2,1,0:T(8,128)}, u32[]{:S(2)}) %copy-start.1) | copy-done | bytes 196632
  5.6 0.0 copy-start.2
  5.6 0.9 %copy-done.2 = f32[24,8,256]{2,1,0:T(8,128)S(1)} copy-done((f32[24,8,256]{2,1,0:T(8,128)S(1)}, f32[24,8,256]{2,1,0:T(8,128)}, u32[]{:S(2)}) %copy-start.2) | copy-done | bytes 196632
  6.5 3.2 %collective-permute-done.h_ref = f32[5,8,256]{2,1,0:T(8,128)S(1)} collective-permute-done((f32[5,8,256]{2,1,0:T(8,128)S(1)}, f32[5,8,256]{2,1,0:T(8,128)S(1)}, u32[]{:S(2)}, u32[]{:S(2)}) %collective-permute-start) | collective-permute-done | bytes 40992 | tf_op jit(solution)/shard_map/ppermute | solution.py:222
  9.7 0.7 %wall.1 = (f32[24,8,256]{2,1,0:T(8,128)S(1)}, f32[34,3,8,256]{3,2,1,0:T(8,128)S(1)}, f32[8,256]{1,0:T(8,128)S(1)}, f32[2,8,256]{2,1,0:T(8,128)S(1)}) custom-call(f32[24,8,256]{2,1,0:T(8,128)S(1)} %get-tuple-element.15.v_ref, f32[24,8,256]{2,1,0:T(8,128)S(1)} %get-tuple-element.14.c_ref, f32[24,8,256]{2,1,0:T(8,128)S(1)} %get-tuple-element.16.e_ref, ...), custom_call_target="tpu_custom_call" | custom-call | tf_op jit(solution)/shard_map/wall/pallas_call | solution.py:233
  10.4 0.1 collective-permute-start.1
  10.5 1.2 %collective-permute-done.1.theirs_ref = f32[8,256]{1,0:T(8,128)S(1)} collective-permute-done((f32[8,256]{1,0:T(8,128)S(1)}, f32[8,256]{1,0:T(8,128)S(1)}, u32[]{:S(2)}, u32[]{:S(2)}) %collective-permute-start.1) | collective-permute-done | bytes 8224 | tf_op jit(solution)/shard_map/ppermute | solution.py:245
  11.6 0.3 %reduce.1 = (f32[5,8,256]{2,1,0:T(8,128)S(1)}, f32[23,3,8,256]{3,2,1,0:T(8,128)S(1)}) custom-call(f32[24,8,256]{2,1,0:T(8,128)S(1)} %get-tuple-element.14.c_ref, f32[5,8,256]{2,1,0:T(8,128)S(1)} %collective-permute-done.h_ref, f32[24,8,256]{2,1,0:T(8,128)S(1)} %get-tuple-element.17.lap_ref, f32[34,3,8,256]{3,2,1,0:T(8,128)S(1)} %get-tuple-element.18.wall_ref, ...), custom_call_target="tpu_custom_call" | custom-call | tf_op jit(solution)/shard_map/reduce/pallas_call | solution.py:246
  12.0 0.1 collective-permute-start.2
  12.1 4.0 %collective-permute-done.2 = f32[5,8,256]{2,1,0:T(8,128)S(1)} collective-permute-done((f32[5,8,256]{2,1,0:T(8,128)S(1)}, f32[5,8,256]{2,1,0:T(8,128)S(1)}, u32[]{:S(2)}, u32[]{:S(2)}) %collective-permute-start.2) | collective-permute-done | bytes 40992 | tf_op jit(solution)/shard_map/ppermute | solution.py:260
  16.2 0.1 collective-permute-start.3
  16.2 4.0 %collective-permute-done.3 = f32[5,8,256]{2,1,0:T(8,128)S(1)} collective-permute-done((f32[5,8,256]{2,1,0:T(8,128)S(1)}, f32[5,8,256]{2,1,0:T(8,128)S(1)}, u32[]{:S(2)}, u32[]{:S(2)}) %collective-permute-start.3) | collective-permute-done | bytes 40992 | tf_op jit(solution)/shard_map/ppermute | solution.py:260
  20.3 0.1 collective-permute-start.4
  20.4 4.0 %collective-permute-done.4 = f32[5,8,256]{2,1,0:T(8,128)S(1)} collective-permute-done((f32[5,8,256]{2,1,0:T(8,128)S(1)}, f32[5,8,256]{2,1,0:T(8,128)S(1)}, u32[]{:S(2)}, u32[]{:S(2)}) %collective-permute-start.4) | collective-permute-done | bytes 40992 | tf_op jit(solution)/shard_map/ppermute | solution.py:260
  24.5 1.3 %collective-permute-start.5 = (f32[5,8,256]{2,1,0:T(8,128)S(1)}, f32[5,8,256]{2,1,0:T(8,128)S(1)}, u32[]{:S(2)}, u32[]{:S(2)}) collective-permute-start(f32[5,8,256]{2,1,0:T(8,128)S(1)} %constant_dynamic-update-slice_fusion.10), channel_id=1, source_target_pairs={{0,16},{2,18},{4,20},{6,22},{8,24},{10,26},{12,28},{14,30},{16,0},... | collective-permute-start | bytes 122888 | tf_op jit(solution)/shard_map/ppermute | solution.py:260
  25.7 3.7 %collective-permute-done.5 = f32[5,8,256]{2,1,0:T(8,128)S(1)} collective-permute-done((f32[5,8,256]{2,1,0:T(8,128)S(1)}, f32[5,8,256]{2,1,0:T(8,128)S(1)}, u32[]{:S(2)}, u32[]{:S(2)}) %collective-permute-start.5) | collective-permute-done | bytes 40992 | tf_op jit(solution)/shard_map/ppermute | solution.py:260
  29.5 0.7 %finish.1 = f32[24,8,256]{2,1,0:T(8,128)} custom-call(f32[23,3,8,256]{3,2,1,0:T(8,128)S(1)} %get-tuple-element.21.joint_ref, f32[2,8,256]{2,1,0:T(8,128)S(1)} %pad_maximum_fusion.1.ends_ref), custom_call_target="tpu_custom_call" | custom-call | tf_op jit(solution)/shard_map/finish/pallas_call | solution.py:274
  (25 shorter events, 0.3 us)
Async XLA Ops:
  0.0 0.7 %slice-start = ((f32[24,8,256]{2,1,0:T(8,128)}), f32[2,8,256]{2,1,0:T(8,128)S(1)}, s32[]{:S(2)}) async-start(f32[24,8,256]{2,1,0:T(8,128)} %v_ref.1), calls=%async_computation | async-start | bytes 32768 | tf_op jit(solution)/shard_map/slice | solution.py:221
  0.0 0.7 %slice-start.1 = ((f32[24,8,256]{2,1,0:T(8,128)}), f32[2,8,256]{2,1,0:T(8,128)S(1)}, s32[]{:S(2)}) async-start(f32[24,8,256]{2,1,0:T(8,128)} %c_ref.1), calls=%async_computation.1 | async-start | bytes 32768 | tf_op jit(solution)/shard_map/slice | solution.py:221
  0.0 0.7 %slice-start.2 = ((f32[24,8,256]{2,1,0:T(8,128)}), f32[1,8,256]{2,1,0:T(8,128)S(1)}, s32[]{:S(2)}) async-start(f32[24,8,256]{2,1,0:T(8,128)} %e_ref.1), calls=%async_computation.2 | async-start | bytes 16384 | tf_op jit(solution)/shard_map/slice | solution.py:221
  0.7 9.0 %collective-permute-start = (f32[5,8,256]{2,1,0:T(8,128)S(1)}, f32[5,8,256]{2,1,0:T(8,128)S(1)}, u32[]{:S(2)}, u32[]{:S(2)}) collective-permute-start(f32[5,8,256]{2,1,0:T(8,128)S(1)} %pad_maximum_fusion), channel_id=1, source_target_pairs={{0,2},{2,4},{4,6},{6,8},{8,10},{10,12},{12,14},{14,16},{16,18},{18... | collective-permute-start | bytes 122888 | tf_op jit(solution)/shard_map/ppermute | solution.py:222
  3.7 0.9 %copy-start = (f32[24,8,256]{2,1,0:T(8,128)S(1)}, f32[24,8,256]{2,1,0:T(8,128)}, u32[]{:S(2)}) copy-start(f32[24,8,256]{2,1,0:T(8,128)} %v_ref.1) | copy-start | bytes 589828
  4.7 0.9 %copy-start.1 = (f32[24,8,256]{2,1,0:T(8,128)S(1)}, f32[24,8,256]{2,1,0:T(8,128)}, u32[]{:S(2)}) copy-start(f32[24,8,256]{2,1,0:T(8,128)} %c_ref.1) | copy-start | bytes 589828
  5.6 0.9 %copy-start.2 = (f32[24,8,256]{2,1,0:T(8,128)S(1)}, f32[24,8,256]{2,1,0:T(8,128)}, u32[]{:S(2)}) copy-start(f32[24,8,256]{2,1,0:T(8,128)} %e_ref.1) | copy-start | bytes 589828
  10.4 1.2 %collective-permute-start.1 = (f32[8,256]{1,0:T(8,128)S(1)}, f32[8,256]{1,0:T(8,128)S(1)}, u32[]{:S(2)}, u32[]{:S(2)}) collective-permute-start(f32[8,256]{1,0:T(8,128)S(1)} %get-tuple-element.20.mine_ref), channel_id=1, source_target_pairs={{0,1},{1,0},{2,3},{3,2},{4,5},{5,4},{6,7},{7,6},{8,9},{9,8},{10,11... | collective-permute-start | bytes 24584 | tf_op jit(solution)/shard_map/ppermute | solution.py:245
  12.0 4.1 %collective-permute-start.2 = (f32[5,8,256]{2,1,0:T(8,128)S(1)}, f32[5,8,256]{2,1,0:T(8,128)S(1)}, u32[]{:S(2)}, u32[]{:S(2)}) collective-permute-start(f32[5,8,256]{2,1,0:T(8,128)S(1)} %get-tuple-element.22), channel_id=1, source_target_pairs={{0,2},{2,0},{4,6},{6,4},{8,10},{10,8},{12,14},{14,12},{16,18},{18,... | collective-permute-start | bytes 122888 | tf_op jit(solution)/shard_map/ppermute | solution.py:260
  16.2 4.1 %collective-permute-start.3 = (f32[5,8,256]{2,1,0:T(8,128)S(1)}, f32[5,8,256]{2,1,0:T(8,128)S(1)}, u32[]{:S(2)}, u32[]{:S(2)}) collective-permute-start(f32[5,8,256]{2,1,0:T(8,128)S(1)} %constant_dynamic-update-slice_fusion), channel_id=1, source_target_pairs={{0,4},{2,6},{4,0},{6,2},{8,12},{10,14},{12,8},{14,10},{16,20},{18,... | collective-permute-start | bytes 122888 | tf_op jit(solution)/shard_map/ppermute | solution.py:260
  20.3 4.1 %collective-permute-start.4 = (f32[5,8,256]{2,1,0:T(8,128)S(1)}, f32[5,8,256]{2,1,0:T(8,128)S(1)}, u32[]{:S(2)}, u32[]{:S(2)}) collective-permute-start(f32[5,8,256]{2,1,0:T(8,128)S(1)} %constant_dynamic-update-slice_fusion.5), channel_id=1, source_target_pairs={{0,8},{2,10},{4,12},{6,14},{8,0},{10,2},{12,4},{14,6},{16,24},{18,... | collective-permute-start | bytes 122888 | tf_op jit(solution)/shard_map/ppermute | solution.py:260
  24.5 5.0 %collective-permute-start.5 = (f32[5,8,256]{2,1,0:T(8,128)S(1)}, f32[5,8,256]{2,1,0:T(8,128)S(1)}, u32[]{:S(2)}, u32[]{:S(2)}) collective-permute-start(f32[5,8,256]{2,1,0:T(8,128)S(1)} %constant_dynamic-update-slice_fusion.10), channel_id=1, source_target_pairs={{0,16},{2,18},{4,20},{6,22},{8,24},{10,26},{12,28},{14,30},{16,0},... | collective-permute-start | bytes 122888 | tf_op jit(solution)/shard_map/ppermute | solution.py:260

commit v3 on v1

v3 whole, which is shorter than its diff:
```python
import functools

import jax
import jax.numpy as jnp
from jax import lax
from jax.experimental import pallas as pl
from jax.experimental.pallas import tpu as pltpu
from jax.sharding import PartitionSpec as P

stream_rate = 1000.0
normal_rate = 50.0
params = pltpu.CompilerParams(vmem_limit_bytes=8 << 20)


def plus(a, b):
    return b if a is None else a if b is None else a + b


def merge(a, b):
    oa, sla, sra, rla, rra = a
    ob, slb, srb, rlb, rrb = b
    sm = plus(sra, slb)
    rm = plus(rra, rlb)
    t = 1.0 / (oa + ob + sm)
    ga = oa * t
    gb = ob * t
    block = (
        oa * gb,
        plus(sla, ga * sm),
        plus(srb, gb * sm),
        plus(rla, ga * rm),
        plus(rrb, gb * rm),
    )
    return block, (t * rm, ga, gb)


def tree_up(lo, hi, leaf, keep):
    if hi - lo == 1:
        return leaf(lo)
    mid = (lo + hi) // 2
    block, joint = merge(tree_up(lo, mid, leaf, keep), tree_up(mid, hi, leaf, keep))
    keep(mid, joint)
    return block


def tree_down(lo, hi, left, right, joint, put):
    if hi - lo == 1:
        return
    mid = (lo + hi) // 2
    z, ga, gb = joint(mid)
    value = z + ga * left + gb * right
    put(mid, value)
    tree_down(lo, mid, left, value, joint, put)
    tree_down(mid, hi, value, right, joint, put)


def load_kernel(v_hbm, c_hbm, e_hbm, v_ref, c_ref, e_ref, sems):
    copies = [
        pltpu.make_async_copy(src, dst, sems.at[n])
        for n, (src, dst) in enumerate(((v_hbm, v_ref), (c_hbm, c_ref), (e_hbm, e_ref)))
    ]
    for copy in copies:
        copy.start()
    for copy in copies:
        copy.wait()


def wall_sweep(start, stop, v_ref, c_ref, e_ref, h_ref, lap_ref, joint_ref, far_ref, rs, cs):
    rows, planes, width = v_ref.shape
    seg = width // 8
    upper = lax.axis_index("gy") == 1
    lower = jnp.logical_not(upper)

    def vel(i):
        return h_ref[0] if i < 0 else v_ref[i]

    def visc(i):
        return h_ref[1] if i < 0 else c_ref[i]

    def face_flux(i):
        if i < -1:
            return h_ref[2]
        return 0.5 * stream_rate * (visc(i) + visc(i + 1)) * (vel(i + 1) - vel(i))

    right_sides, coefs = [], []
    west = face_flux(start - 1)
    for i in range(start, stop):
        east = face_flux(i)
        lap = east - west
        lap_ref[i - start] = lap
        right_sides.append(h_ref[3] + east if i < 0 else v_ref[i] + lap + e_ref[i])
        coefs.append(visc(i))
        west = east
    spare = -len(coefs) % (128 // planes)
    turn(right_sides + (right_sides * spare)[:spare], rs)
    turn(coefs + (coefs * spare)[:spare], cs)

    def load(ref, m):
        return jnp.concatenate(
            [ref[n, pl.ds(m, 8, stride=seg), :] for n in range(ref.shape[0])], axis=1
        )

    sub = lax.broadcasted_iota(jnp.int32, (8, rs.shape[0] * 128), 0)
    one = jnp.ones(sub.shape, jnp.float32)
    c_first = load(cs, 0)
    c_last = load(cs, seg - 1)
    s_first = one + jnp.where((sub == 0) & lower, normal_rate * c_first, 0.0)
    s_last = one + jnp.where((sub == 7) & upper, normal_rate * c_last, 0.0)

    def leaf(m):
        o = 0.5 * normal_rate * (load(cs, m) + load(cs, m + 1))
        s = s_first if m == 0 else one
        if m == seg - 2:
            return (o, s, s_last, load(rs, m), load(rs, m + 1))
        return (o, s, None, load(rs, m), None)

    def keep(m, joint):
        for n in range(3):
            joint_ref[m - 1, n] = joint[n]

    block = tree_up(0, seg - 1, leaf, keep)
    link = 0.5 * normal_rate * (c_last + pltpu.roll(c_first, 7, 0))
    zero = jnp.zeros_like(one)
    linked, joint = merge(block, (link, None, zero, None, zero))
    last = sub == 7
    block = tuple(jnp.where(last, x, y) for x, y in zip(block, linked))
    keep(seg - 1, tuple(jnp.where(last, x, y) for x, y in zip((zero, zero, one), joint)))
    for n, h in enumerate((1, 2, 4)):
        block, joint = merge(block, tuple(pltpu.roll(x, 8 - h, 0) for x in block))
        keep(seg + n, joint)
    o, sl, sr, rl, rr = block
    s_far = jnp.where(upper, sr, sl)
    s_near = jnp.where(upper, sl, sr)
    r_far = jnp.where(upper, rr, rl)
    r_near = jnp.where(upper, rl, rr)
    t = 1.0 / (o + s_far)
    c_edge = jnp.where(upper, c_first, pltpu.roll(c_last, 1, 0))
    ot = o * t
    far_ref[0] = t * r_far
    far_ref[1] = ot
    return jnp.where(
        sub == 0,
        s_near + ot * s_far,
        jnp.where(sub == 1, pltpu.roll(r_near + ot * r_far, 1, 0), pltpu.roll(c_edge, 2, 0)),
    )


def turn(blocks, ref):
    per = 128 // blocks[0].shape[0]
    for n in range(ref.shape[0]):
        ref[n] = jnp.concatenate(blocks[n * per : (n + 1) * per], axis=0).T


def inner_kernel(start, v_ref, c_ref, e_ref, lap_ref, joint_ref, edge_ref, far_ref, rs, cs):
    edge_ref[...] = wall_sweep(
        start, v_ref.shape[0] - 1, v_ref, c_ref, e_ref, None, lap_ref, joint_ref, far_ref, rs, cs
    )


def outer_kernel(
    stop, v_ref, c_ref, e_ref, h_ref, inner_ref, lap_ref, joint_ref, edge_ref, far_ref, rs, cs
):
    edge = wall_sweep(
        -1, stop, v_ref, c_ref, e_ref, h_ref, lap_ref, joint_ref, far_ref, rs, cs
    )
    edge_ref[...] = jnp.concatenate([edge, inner_ref[...]], axis=1)


def reduce_kernel(
    c_ref,
    h_ref,
    lap_a,
    lap_b,
    wall_a,
    wall_b,
    far_a,
    far_b,
    mine_ref,
    theirs_ref,
    block_ref,
    joint_ref,
    ps,
):
    rows, planes, width = c_ref.shape
    seg = width // 8
    split = far_a.shape[2]
    upper = lax.axis_index("gy") == 1
    s0, r0, c0 = (mine_ref[n : n + 1] for n in range(3))
    s1, r1, c1 = (theirs_ref[n : n + 1] for n in range(3))
    face = 0.5 * normal_rate * (c0 + c1)
    ft = face / (s1 + face)
    near_all = (r0 + ft * r1) / (s0 + ft * s1)
    turned = []
    for at, wall_ref, far_ref in ((0, wall_a, far_a), (split, wall_b, far_b)):
        lanes = far_ref.shape[2]
        near = jnp.broadcast_to(near_all[:, at : at + lanes], (8, lanes))
        far = far_ref[0] + far_ref[1] * near
        left = jnp.where(upper, near, far)
        right = jnp.where(upper, far, near)
        sub = lax.broadcasted_iota(jnp.int32, left.shape, 0)

        def wall_joint(m, wall_ref=wall_ref):
            return tuple(wall_ref[m - 1, n] for n in range(3))

        for n, h in ((2, 4), (1, 2), (0, 1)):
            z, ga, gb = wall_joint(seg + n)
            mid = z + ga * left + gb * right
            fresh = (sub & h) != 0
            left, right = (
                jnp.where(fresh, pltpu.roll(mid, h, 0), left),
                jnp.where(fresh, pltpu.roll(right, h, 0), mid),
            )

        def put(m, value, at=at, lanes=lanes):
            for n in range(lanes // 128):
                ps[at // 128 + n, pl.ds(m, 8, stride=seg), :] = value[:, n * 128 : n * 128 + 128]

        put(0, left)
        z, ga, gb = wall_joint(seg - 1)
        end = z + ga * left + gb * right
        put(seg - 1, end)
        tree_down(0, seg - 1, left, end, wall_joint, put)
        turned += [ps[at // 128 + n].T for n in range(lanes // 128)]
    first = lap_a.shape[0]

    def visc(i):
        return h_ref[1] if i < 0 else c_ref[i]

    def leaf(r):
        lap = lap_a[r] if r < first else lap_b[r - first]
        at = r * planes if r < first else split + (r - first) * planes
        q = turned[at // 128][at % 128 : at % 128 + planes] - lap
        o = 0.5 * stream_rate * (visc(r - 1) + visc(r))
        return (o, jnp.ones_like(q), None, q, None)

    def keep(m, joint):
        for n in range(3):
            joint_ref[m - 1, n] = joint[n]

    whole = tree_up(0, rows, leaf, keep)
    for n in range(5):
        block_ref[n] = whole[n]


def join(bit, mine_ref, theirs_ref):
    right = (lax.axis_index("gx") & bit) != 0
    a, b = [], []
    for n in range(5):
        mine, theirs = mine_ref[n], theirs_ref[n]
        a.append(jnp.where(right, theirs, mine))
        b.append(jnp.where(right, mine, theirs))
    return right, *merge(a, b)


def join_kernel(bit, mine_ref, theirs_ref, block_ref, joint_ref):
    _, block, joint = join(bit, mine_ref, theirs_ref)
    for n in range(5):
        block_ref[n] = block[n]
    for n in range(3):
        joint_ref[n] = joint[n]


def finish_kernel(bits, joint_ref, mine_ref, theirs_ref, *refs):
    out_ref = refs[-1]
    rows = out_ref.shape[0]
    right, (_, sl, sr, rl, rr), (z, ga, gb) = join(bits[-1], mine_ref, theirs_ref)
    low = (rl + rr) / (sl + sr)
    mid = z + (ga + gb) * low
    low, high = jnp.where(right, mid, low), jnp.where(right, low, mid)
    for bit, ref in zip(bits[-2::-1], refs[-2::-1]):
        right = (lax.axis_index("gx") & bit) != 0
        mid = ref[0] + ref[1] * low + ref[2] * high
        low, high = jnp.where(right, mid, low), jnp.where(right, high, mid)

    def joint(m):
        return tuple(joint_ref[m - 1, n] for n in range(3))

    def put(m, value):
        out_ref[m - 1] = value

    put(rows, high)
    tree_down(0, rows, low, high, joint, put)


def per_device(velocity, viscosity, explicit):
    rows, planes, width = velocity.shape
    count = lax.axis_size("gx")
    seg = width // 8
    per = 128 // planes
    tiles = -(-rows // per)
    inside = (tiles - 1) * per
    outside = rows - inside

    def array(*shape):
        return jax.ShapeDtypeStruct(shape, jnp.float32)

    def cost(size):
        return pl.CostEstimate(flops=0, bytes_accessed=size, transcendentals=0)

    field = array(rows, planes, width)
    block_shape = array(5, planes, width)
    tail_v, tail_c, tail_e = velocity[-2:], viscosity[-2:], explicit[-1]
    flux = 0.5 * stream_rate * (tail_c[0] + tail_c[1]) * (tail_v[1] - tail_v[0])
    message = jnp.stack([tail_v[1], tail_c[1], flux, tail_v[1] + tail_e - flux])
    halo = lax.ppermute(message, "gx", [(i, (i + 1) % count) for i in range(count)])
    v, c, e = pl.pallas_call(
        load_kernel,
        out_shape=[field] * 3,
        in_specs=[pl.BlockSpec(memory_space=pltpu.HBM)] * 3,
        scratch_shapes=[pltpu.SemaphoreType.DMA((3,))],
        compiler_params=params,
        cost_estimate=cost(8 << 20),
        name="load",
    )(*(pltpu.with_memory_space_constraint(x, pltpu.HBM) for x in (velocity, viscosity, explicit)))
    lap_b, wall_b, edge_b, far_b = pl.pallas_call(
        functools.partial(inner_kernel, outside - 1),
        out_shape=[
            array(inside, planes, width),
            array(seg + 2, 3, 8, (tiles - 1) * 128),
            array(8, (tiles - 1) * 128),
            array(2, 8, (tiles - 1) * 128),
        ],
        scratch_shapes=[pltpu.VMEM((tiles - 1, width, 128), jnp.float32)] * 2,
        compiler_params=params,
        cost_estimate=cost(8 << 20),
        name="inner",
    )(v, c, e)
    lap_a, wall_a, edge, far_a = pl.pallas_call(
        functools.partial(outer_kernel, outside - 1),
        out_shape=[
            array(outside, planes, width),
            array(seg + 2, 3, 8, 128),
            array(8, tiles * 128),
            array(2, 8, 128),
        ],
        scratch_shapes=[pltpu.VMEM((1, width, 128), jnp.float32)] * 2,
        compiler_params=params,
        name="outer",
    )(v, c, e, halo, edge_b)
    other = lax.ppermute(edge, "gy", [(0, 1), (1, 0)])
    block, joints = pl.pallas_call(
        reduce_kernel,
        out_shape=[block_shape, array(rows - 1, 3, planes, width)],
        scratch_shapes=[pltpu.VMEM((tiles, width, 128), jnp.float32)],
        compiler_params=params,
        name="reduce",
    )(c, halo, lap_a, lap_b, wall_a, wall_b, far_a, far_b, edge, other)
    bits = [1 << n for n in range(count.bit_length() - 1)]
    path = []
    for bit in bits:
        partner = lax.ppermute(block, "gx", [(i, i ^ bit) for i in range(count)])
        if bit != bits[-1]:
            block, joint = pl.pallas_call(
                functools.partial(join_kernel, bit),
                out_shape=[block_shape, array(3, planes, width)],
                compiler_params=params,
                name=f"join_{bit}",
            )(block, partner)
            path.append(joint)
    return pl.pallas_call(
        functools.partial(finish_kernel, bits),
        out_shape=field,
        compiler_params=params,
        name="finish",
    )(joints, block, partner, *path)


def solution(mesh):
    return jax.shard_map(
        per_device,
        mesh=mesh,
        in_specs=(P("gx", None, "gy"), P("gx", None, "gy"), P("gx", None, "gy")),
        out_specs=P("gx", None, "gy"),
        check_vma=False,
    )
```

time: 38.6 us -> 29.8 us (0.77)
  Pallas kernels: 6.93 us -> 2.96 us
  waiting for transfers between devices: 23.2 us -> 21.2 us
  local copies, waits for them, and re-layouts: 1.94 us -> 0 us
  other arithmetic: 1.61 us -> 0.77 us
    pallas_call x3 -> x8, Pallas kernels: 6.93 us -> 2.96 us  [the longest x1 1.14 us: per_device(): pl.pallas_call(load_kernel, out_shape=[field] * 3, in_specs=[pl.BlockSpec...]
    ppermute x1, waiting for transfers between devices: 5.97 us -> 4.4 us  [per_device(): lax.ppermute(message, 'gx', [(i, (i + 1) % count) for i in range(count)])]
    unnamed x4 -> x0, local copies, waits for them, and re-layouts: 1.21 us -> none
    select_n x6 -> x0, other arithmetic: 0.85 us -> none  [the longest x3 0.8 us: per_device(): b = jnp.where(right, block, partner)]
    sub x0 -> x1, other arithmetic: none -> 0.77 us  [per_device(): message = jnp.stack([tail_v[1], tail_c[1], flux, tail_v[1] + tail_e - flux])]
    slice x6 -> x0, local copies, waits for them, and re-layouts: 0.73 us -> none  [the longest x2 0.71 us: per_device(): viscosity[-2:]]
    another operation x4 -> x1, other arithmetic: 0.63 us -> 0.01 us  [per_device(): message = jnp.stack([tail_v[1], tail_c[1], flux, tail_v[1] + tail_e - flux])]
  transfers between devices with their start and end apart: 6 -> 6, of which waited for: 6 -> 6; matrix products, arithmetic and copies ran while one was open for 0% -> 0% of each run, Pallas kernels for 0% -> 5%
where the time goes in v3:
time: 29.8 us; the launch traced here: 29.6 us
  waiting for transfers between devices  21.2 us (71%)
  starting transfers between devices  4.6 us (15%)
  Pallas kernels  2.96 us (10%)
  other arithmetic  0.77 us (3%)
    ppermute x4, waiting for transfers between devices, per_device(): partner = lax.ppermute(block, 'gx', [(i, i ^ bit) for i in range(count)])  15.6 us
    ppermute x1, waiting for transfers between devices, per_device(): lax.ppermute(message, 'gx', [(i, (i + 1) % count) for i in range(count)])  4.4 us
    ppermute x1, starting transfers between devices, per_device(): lax.ppermute(message, 'gx', [(i, (i + 1) % count) for i in range(count)])  2.99 us
    ppermute x4, starting transfers between devices, per_device(): partner = lax.ppermute(block, 'gx', [(i, i ^ bit) for i in range(count)])  1.54 us
    ppermute x1, waiting for transfers between devices, per_device(): other = lax.ppermute(edge, 'gy', [(0, 1), (1, 0)])  1.16 us
    pallas_call x1, Pallas kernels, per_device(): pl.pallas_call(load_kernel, out_shape=[field] * 3, in_specs=[pl.BlockSpec...  1.14 us
    sub x1, other arithmetic, per_device(): message = jnp.stack([tail_v[1], tail_c[1], flux, tail_v[1] + tail_e - flux])  0.77 us
    pallas_call x1, Pallas kernels, per_device(): pl.pallas_call(functools.partial(finish_kernel, bits), out_shape=field, c...  0.74 us
  transfers between devices with their start and end apart: 6, of which 6 were waited for; matrix products, arithmetic and copies ran while one was open for 0% of the time, Pallas kernels for 5%

profile of v3, /device:TPU:0, one launch (start us, length us, event | category | flops | bytes accessed | tf_op | source)
XLA Modules:
  0.0 29.6 jit_solution(11957098225471588443)
XLA Ops:
  0.0 0.8 %add_subtract_fusion = (f32[1,8,256]{2,1,0:T(8,128)S(1)}, f32[1,8,256]{2,1,0:T(8,128)S(1)}, f32[1,8,256]{2,1,0:T(8,128)S(1)}, f32[1,8,256]{2,1,0:T(8,128)S(1)}) fusion(f32[24,8,256]{2,1,0:T(8,128)} %e_hbm.1, f32[24,8,256]{2,1,0:T(8,128)} %v_hbm.1, f32[24,8,256]{2,1,0:T(8,128)} %c_hbm.1), kind=kLoop, calls=%fused_computation.1 | loop fusion | flops 12288 | bytes 73728 | tf_op jit(solution)/shard_map/sub | solution.py:304
  0.8 3.0 %collective-permute-start = (f32[4,8,256]{2,1,0:T(8,128)S(1)}, f32[4,8,256]{2,1,0:T(8,128)S(1)}, u32[]{:S(2)}, u32[]{:S(2)}) collective-permute-start(f32[4,8,256]{2,1,0:T(8,128)S(1)} %pad_maximum_fusion), channel_id=1, source_target_pairs={{0,2},{2,4},{4,6},{6,8},{8,10},{10,12},{12,14},{14,16},{16,18},{18... | collective-permute-start | bytes 98312 | tf_op jit(solution)/shard_map/ppermute | solution.py:305
  3.8 1.1 %load.1 = (f32[24,8,256]{2,1,0:T(8,128)S(1)}, f32[24,8,256]{2,1,0:T(8,128)S(1)}, f32[24,8,256]{2,1,0:T(8,128)S(1)}) custom-call(f32[24,8,256]{2,1,0:T(8,128)} %v_hbm.1, f32[24,8,256]{2,1,0:T(8,128)} %c_hbm.1, f32[24,8,256]{2,1,0:T(8,128)} %e_hbm.1), custom_call_target="tpu_custom_call" | custom-call | bytes 8388608 | tf_op jit(solution)/shard_map/load/pallas_call | solution.py:306
  4.9 0.3 %inner.1 = (f32[16,8,256]{2,1,0:T(8,128)S(1)}, f32[34,3,8,128]{3,2,1,0:T(8,128)S(1)}, f32[8,128]{1,0:T(8,128)S(1)}, f32[2,8,128]{2,1,0:T(8,128)S(1)}) custom-call(f32[24,8,256]{2,1,0:T(8,128)S(1)} %get-tuple-element.25.v_ref, f32[24,8,256]{2,1,0:T(8,128)S(1)} %get-tuple-element.24.c_ref, f32[24,8,256]{2,1,0:T(8,128)S(1)} %get-tuple-element.26.e_ref), custom_call_target="tpu_custom_call" | custom-call | bytes 8388608 | tf_op jit(solution)/shard_map/inner/pallas_call | solution.py:315
  5.3 4.4 %collective-permute-done.h_ref = f32[4,8,256]{2,1,0:T(8,128)S(1)} collective-permute-done((f32[4,8,256]{2,1,0:T(8,128)S(1)}, f32[4,8,256]{2,1,0:T(8,128)S(1)}, u32[]{:S(2)}, u32[]{:S(2)}) %collective-permute-start) | collective-permute-done | bytes 32800 | tf_op jit(solution)/shard_map/ppermute | solution.py:305
  9.7 0.3 %outer.1 = (f32[8,8,256]{2,1,0:T(8,128)S(1)}, f32[34,3,8,128]{3,2,1,0:T(8,128)S(1)}, f32[8,256]{1,0:T(8,128)S(1)}, f32[2,8,128]{2,1,0:T(8,128)S(1)}) custom-call(f32[24,8,256]{2,1,0:T(8,128)S(1)} %get-tuple-element.25.v_ref, f32[24,8,256]{2,1,0:T(8,128)S(1)} %get-tuple-element.24.c_ref, f32[24,8,256]{2,1,0:T(8,128)S(1)} %get-tuple-element.26.e_ref, ...), custom_call_target="tpu_custom_call" | custom-call | tf_op jit(solution)/shard_map/outer/pallas_call | solution.py:328
  10.0 0.1 collective-permute-start.1
  10.1 1.2 %collective-permute-done.1.theirs_ref = f32[8,256]{1,0:T(8,128)S(1)} collective-permute-done((f32[8,256]{1,0:T(8,128)S(1)}, f32[8,256]{1,0:T(8,128)S(1)}, u32[]{:S(2)}, u32[]{:S(2)}) %collective-permute-start.1) | collective-permute-done | bytes 8224 | tf_op jit(solution)/shard_map/ppermute | solution.py:340
  11.2 0.4 %reduce.1 = (f32[5,8,256]{2,1,0:T(8,128)S(1)}, f32[23,3,8,256]{3,2,1,0:T(8,128)S(1)}) custom-call(f32[24,8,256]{2,1,0:T(8,128)S(1)} %get-tuple-element.24.c_ref, f32[4,8,256]{2,1,0:T(8,128)S(1)} %collective-permute-done.h_ref, f32[8,8,256]{2,1,0:T(8,128)S(1)} %get-tuple-element.28.lap_a, f32[16,8,256]{2,1,0:T(8,128)S(1)} %get-tuple-element.29.lap_b, ...), custom_call_target="tpu_custom_call" | custom-call | tf_op jit(solution)/shard_map/reduce/pallas_call | solution.py:341
  11.6 0.1 collective-permute-start.2
  11.7 4.0 %collective-permute-done.2.theirs_ref = f32[5,8,256]{2,1,0:T(8,128)S(1)} collective-permute-done((f32[5,8,256]{2,1,0:T(8,128)S(1)}, f32[5,8,256]{2,1,0:T(8,128)S(1)}, u32[]{:S(2)}, u32[]{:S(2)}) %collective-permute-start.2) | collective-permute-done | bytes 40992 | tf_op jit(solution)/shard_map/ppermute | solution.py:351
  15.7 0.1 collective-permute-start.3
  15.8 4.0 %collective-permute-done.3.theirs_ref = f32[5,8,256]{2,1,0:T(8,128)S(1)} collective-permute-done((f32[5,8,256]{2,1,0:T(8,128)S(1)}, f32[5,8,256]{2,1,0:T(8,128)S(1)}, u32[]{:S(2)}, u32[]{:S(2)}) %collective-permute-start.3) | collective-permute-done | bytes 40992 | tf_op jit(solution)/shard_map/ppermute | solution.py:351
  19.8 0.1 collective-permute-start.4
  19.9 4.0 %collective-permute-done.4.theirs_ref = f32[5,8,256]{2,1,0:T(8,128)S(1)} collective-permute-done((f32[5,8,256]{2,1,0:T(8,128)S(1)}, f32[5,8,256]{2,1,0:T(8,128)S(1)}, u32[]{:S(2)}, u32[]{:S(2)}) %collective-permute-start.4) | collective-permute-done | bytes 40992 | tf_op jit(solution)/shard_map/ppermute | solution.py:351
  23.9 1.3 %collective-permute-start.5 = (f32[5,8,256]{2,1,0:T(8,128)S(1)}, f32[5,8,256]{2,1,0:T(8,128)S(1)}, u32[]{:S(2)}, u32[]{:S(2)}) collective-permute-start(f32[5,8,256]{2,1,0:T(8,128)S(1)} %get-tuple-element.39.mine_ref), channel_id=1, source_target_pairs={{0,16},{2,18},{4,20},{6,22},{8,24},{10,26},{12,28},{14,30},{16,0},... | collective-permute-start | bytes 122888 | tf_op jit(solution)/shard_map/ppermute | solution.py:351
  25.2 3.6 %collective-permute-done.5.theirs_ref = f32[5,8,256]{2,1,0:T(8,128)S(1)} collective-permute-done((f32[5,8,256]{2,1,0:T(8,128)S(1)}, f32[5,8,256]{2,1,0:T(8,128)S(1)}, u32[]{:S(2)}, u32[]{:S(2)}) %collective-permute-start.5) | collective-permute-done | bytes 40992 | tf_op jit(solution)/shard_map/ppermute | solution.py:351
  28.8 0.7 %finish.1 = f32[24,8,256]{2,1,0:T(8,128)} custom-call(f32[23,3,8,256]{3,2,1,0:T(8,128)S(1)} %get-tuple-element.35.joint_ref, f32[5,8,256]{2,1,0:T(8,128)S(1)} %get-tuple-element.39.mine_ref, f32[5,8,256]{2,1,0:T(8,128)S(1)} %collective-permute-done.5.theirs_ref, f32[3,8,256]{2,1,0:T(8,128)S(1)} %get-tuple-element.40.refs_0_, ...), custom_call_target="tpu_custom_call" | custom-call | tf_op jit(solution)/shard_map/finish/pallas_call | solution.py:360
  (4 shorter events, 0.1 us)
Async XLA Ops:
  0.8 8.9 %collective-permute-start = (f32[4,8,256]{2,1,0:T(8,128)S(1)}, f32[4,8,256]{2,1,0:T(8,128)S(1)}, u32[]{:S(2)}, u32[]{:S(2)}) collective-permute-start(f32[4,8,256]{2,1,0:T(8,128)S(1)} %pad_maximum_fusion), channel_id=1, source_target_pairs={{0,2},{2,4},{4,6},{6,8},{8,10},{10,12},{12,14},{14,16},{16,18},{18... | collective-permute-start | bytes 98312 | tf_op jit(solution)/shard_map/ppermute | solution.py:305
  10.0 1.2 %collective-permute-start.1 = (f32[8,256]{1,0:T(8,128)S(1)}, f32[8,256]{1,0:T(8,128)S(1)}, u32[]{:S(2)}, u32[]{:S(2)}) collective-permute-start(f32[8,256]{1,0:T(8,128)S(1)} %get-tuple-element.34.mine_ref), channel_id=1, source_target_pairs={{0,1},{1,0},{2,3},{3,2},{4,5},{5,4},{6,7},{7,6},{8,9},{9,8},{10,11... | collective-permute-start | bytes 24584 | tf_op jit(solution)/shard_map/ppermute | solution.py:340
  11.6 4.1 %collective-permute-start.2 = (f32[5,8,256]{2,1,0:T(8,128)S(1)}, f32[5,8,256]{2,1,0:T(8,128)S(1)}, u32[]{:S(2)}, u32[]{:S(2)}) collective-permute-start(f32[5,8,256]{2,1,0:T(8,128)S(1)} %get-tuple-element.36.mine_ref), channel_id=1, source_target_pairs={{0,2},{2,0},{4,6},{6,4},{8,10},{10,8},{12,14},{14,12},{16,18},{18,... | collective-permute-start | bytes 122888 | tf_op jit(solution)/shard_map/ppermute | solution.py:351
  15.7 4.1 %collective-permute-start.3 = (f32[5,8,256]{2,1,0:T(8,128)S(1)}, f32[5,8,256]{2,1,0:T(8,128)S(1)}, u32[]{:S(2)}, u32[]{:S(2)}) collective-permute-start(f32[5,8,256]{2,1,0:T(8,128)S(1)} %get-tuple-element.37.mine_ref), channel_id=1, source_target_pairs={{0,4},{2,6},{4,0},{6,2},{8,12},{10,14},{12,8},{14,10},{16,20},{18,... | collective-permute-start | bytes 122888 | tf_op jit(solution)/shard_map/ppermute | solution.py:351
  19.8 4.1 %collective-permute-start.4 = (f32[5,8,256]{2,1,0:T(8,128)S(1)}, f32[5,8,256]{2,1,0:T(8,128)S(1)}, u32[]{:S(2)}, u32[]{:S(2)}) collective-permute-start(f32[5,8,256]{2,1,0:T(8,128)S(1)} %get-tuple-element.38.mine_ref), channel_id=1, source_target_pairs={{0,8},{2,10},{4,12},{6,14},{8,0},{10,2},{12,4},{14,6},{16,24},{18,... | collective-permute-start | bytes 122888 | tf_op jit(solution)/shard_map/ppermute | solution.py:351
  23.9 5.0 %collective-permute-start.5 = (f32[5,8,256]{2,1,0:T(8,128)S(1)}, f32[5,8,256]{2,1,0:T(8,128)S(1)}, u32[]{:S(2)}, u32[]{:S(2)}) collective-permute-start(f32[5,8,256]{2,1,0:T(8,128)S(1)} %get-tuple-element.39.mine_ref), channel_id=1, source_target_pairs={{0,16},{2,18},{4,20},{6,22},{8,24},{10,26},{12,28},{14,30},{16,0},... | collective-permute-start | bytes 122888 | tf_op jit(solution)/shard_map/ppermute | solution.py:351

commit v4 on v3

--- a/solution.py
+++ b/solution.py
@@ -252,6 +252,27 @@
     return right, *merge(a, b)
 
 
+def group_kernel(all_ref, block_ref, *joint_refs):
+    blocks = [tuple(all_ref[m, n] for n in range(5)) for m in range(all_ref.shape[0])]
+    place = lax.axis_index("gx") & (len(blocks) - 1)
+    for level, ref in enumerate(joint_refs):
+        merged = [merge(blocks[m], blocks[m + 1]) for m in range(0, len(blocks), 2)]
+        blocks = [block for block, _ in merged]
+        joints = [joint for _, joint in merged]
+        bit = 1 << level
+        while len(joints) > 1:
+            bit *= 2
+            upper = (place & bit) != 0
+            joints = [
+                tuple(jnp.where(upper, y, x) for x, y in zip(joints[m], joints[m + 1]))
+                for m in range(0, len(joints), 2)
+            ]
+        for n in range(3):
+            ref[n] = joints[0][n]
+    for n in range(5):
+        block_ref[n] = blocks[0][n]
+
+
 def join_kernel(bit, mine_ref, theirs_ref, block_ref, joint_ref):
     _, block, joint = join(bit, mine_ref, theirs_ref)
     for n in range(5):
@@ -346,8 +367,22 @@
         name="reduce",
     )(c, halo, lap_a, lap_b, wall_a, wall_b, far_a, far_b, edge, other)
     bits = [1 << n for n in range(count.bit_length() - 1)]
-    path = []
-    for bit in bits:
+    group = 1 << min(3, len(bits) - 1)
+    everyone = lax.all_to_all(
+        jnp.broadcast_to(block[None], (group,) + block.shape),
+        "gx",
+        0,
+        0,
+        tiled=True,
+        axis_index_groups=[list(range(i, i + group)) for i in range(0, count, group)],
+    )
+    block, *path = pl.pallas_call(
+        group_kernel,
+        out_shape=[block_shape] + [array(3, planes, width)] * (group.bit_length() - 1),
+        compiler_params=params,
+        name="group",
+    )(everyone)
+    for bit in bits[group.bit_length() - 1 :]:
         partner = lax.ppermute(block, "gx", [(i, i ^ bit) for i in range(count)])
         if bit != bits[-1]:
             block, joint = pl.pallas_call(

time: 29.8 us -> 28.6 us (0.960)
  waiting for transfers between devices: 21.2 us -> 9.91 us
  blocking collectives: 0 us -> 10.6 us
  starting transfers between devices: 4.6 us -> 4.12 us
    ppermute x4 -> x1, waiting for transfers between devices: 15.6 us -> 4.35 us  [per_device(): partner = lax.ppermute(block, 'gx', [(i, i ^ bit) for i in range(count)])]
    all_to_all x0 -> x1, blocking collectives: none -> 10.6 us  [per_device(): lax.all_to_all(jnp.broadcast_to(block[None], (group,) + block.shape), 'gx...]
    ppermute x4 -> x1, starting transfers between devices: 1.54 us -> 1.06 us  [per_device(): partner = lax.ppermute(block, 'gx', [(i, i ^ bit) for i in range(count)])]
  transfers between devices with their start and end apart: 6 -> 3, of which waited for: 6 -> 3; matrix products, arithmetic and copies ran while one was open for 0% -> 0% of each run, Pallas kernels for 5% -> 5%
where the time goes in v4:
time: 28.6 us; the launch traced here: 28.4 us
  blocking collectives  10.6 us (37%)
  waiting for transfers between devices  9.91 us (35%)
  starting transfers between devices  4.12 us (14%)
  Pallas kernels  2.94 us (10%)
  other arithmetic  0.77 us (3%)
    all_to_all x1, blocking collectives, per_device(): lax.all_to_all(jnp.broadcast_to(block[None], (group,) + block.shape), 'gx...  10.6 us
    ppermute x1, waiting for transfers between devices, per_device(): lax.ppermute(message, 'gx', [(i, (i + 1) % count) for i in range(count)])  4.41 us
    ppermute x1, waiting for transfers between devices, per_device(): partner = lax.ppermute(block, 'gx', [(i, i ^ bit) for i in range(count)])  4.35 us
    ppermute x1, starting transfers between devices, per_device(): lax.ppermute(message, 'gx', [(i, (i + 1) % count) for i in range(count)])  2.99 us
    ppermute x1, waiting for transfers between devices, per_device(): other = lax.ppermute(edge, 'gy', [(0, 1), (1, 0)])  1.16 us
    pallas_call x1, Pallas kernels, per_device(): pl.pallas_call(load_kernel, out_shape=[field] * 3, in_specs=[pl.BlockSpec...  1.14 us
    ppermute x1, starting transfers between devices, per_device(): partner = lax.ppermute(block, 'gx', [(i, i ^ bit) for i in range(count)])  1.06 us
    sub x1, other arithmetic, per_device(): message = jnp.stack([tail_v[1], tail_c[1], flux, tail_v[1] + tail_e - flux])  0.77 us
  transfers between devices with their start and end apart: 3, of which 3 were waited for; matrix products, arithmetic and copies ran while one was open for 0% of the time, Pallas kernels for 5%

profile of v4, /device:TPU:0, one launch (start us, length us, event | category | flops | bytes accessed | tf_op | source)
XLA Modules:
  0.0 28.4 jit_solution(12608183778502897031)
XLA Ops:
  0.0 0.8 %add_subtract_fusion = (f32[1,8,256]{2,1,0:T(8,128)S(1)}, f32[1,8,256]{2,1,0:T(8,128)S(1)}, f32[1,8,256]{2,1,0:T(8,128)S(1)}, f32[1,8,256]{2,1,0:T(8,128)S(1)}) fusion(f32[24,8,256]{2,1,0:T(8,128)} %e_hbm.1, f32[24,8,256]{2,1,0:T(8,128)} %v_hbm.1, f32[24,8,256]{2,1,0:T(8,128)} %c_hbm.1), kind=kLoop, calls=%fused_computation.1 | loop fusion | flops 12288 | bytes 73728 | tf_op jit(solution)/shard_map/sub | solution.py:325
  0.8 3.0 %collective-permute-start = (f32[4,8,256]{2,1,0:T(8,128)S(1)}, f32[4,8,256]{2,1,0:T(8,128)S(1)}, u32[]{:S(2)}, u32[]{:S(2)}) collective-permute-start(f32[4,8,256]{2,1,0:T(8,128)S(1)} %pad_maximum_fusion), channel_id=1, source_target_pairs={{0,2},{2,4},{4,6},{6,8},{8,10},{10,12},{12,14},{14,16},{16,18},{18... | collective-permute-start | bytes 98312 | tf_op jit(solution)/shard_map/ppermute | solution.py:326
  3.8 1.1 %load.1 = (f32[24,8,256]{2,1,0:T(8,128)S(1)}, f32[24,8,256]{2,1,0:T(8,128)S(1)}, f32[24,8,256]{2,1,0:T(8,128)S(1)}) custom-call(f32[24,8,256]{2,1,0:T(8,128)} %v_hbm.1, f32[24,8,256]{2,1,0:T(8,128)} %c_hbm.1, f32[24,8,256]{2,1,0:T(8,128)} %e_hbm.1), custom_call_target="tpu_custom_call" | custom-call | bytes 8388608 | tf_op jit(solution)/shard_map/load/pallas_call | solution.py:327
  4.9 0.3 %inner.1 = (f32[16,8,256]{2,1,0:T(8,128)S(1)}, f32[34,3,8,128]{3,2,1,0:T(8,128)S(1)}, f32[8,128]{1,0:T(8,128)S(1)}, f32[2,8,128]{2,1,0:T(8,128)S(1)}) custom-call(f32[24,8,256]{2,1,0:T(8,128)S(1)} %get-tuple-element.23.v_ref, f32[24,8,256]{2,1,0:T(8,128)S(1)} %get-tuple-element.22.c_ref, f32[24,8,256]{2,1,0:T(8,128)S(1)} %get-tuple-element.24.e_ref), custom_call_target="tpu_custom_call" | custom-call | bytes 8388608 | tf_op jit(solution)/shard_map/inner/pallas_call | solution.py:336
  5.2 4.4 %collective-permute-done.h_ref = f32[4,8,256]{2,1,0:T(8,128)S(1)} collective-permute-done((f32[4,8,256]{2,1,0:T(8,128)S(1)}, f32[4,8,256]{2,1,0:T(8,128)S(1)}, u32[]{:S(2)}, u32[]{:S(2)}) %collective-permute-start) | collective-permute-done | bytes 32800 | tf_op jit(solution)/shard_map/ppermute | solution.py:326
  9.7 0.3 %outer.1 = (f32[8,8,256]{2,1,0:T(8,128)S(1)}, f32[34,3,8,128]{3,2,1,0:T(8,128)S(1)}, f32[8,256]{1,0:T(8,128)S(1)}, f32[2,8,128]{2,1,0:T(8,128)S(1)}) custom-call(f32[24,8,256]{2,1,0:T(8,128)S(1)} %get-tuple-element.23.v_ref, f32[24,8,256]{2,1,0:T(8,128)S(1)} %get-tuple-element.22.c_ref, f32[24,8,256]{2,1,0:T(8,128)S(1)} %get-tuple-element.24.e_ref, ...), custom_call_target="tpu_custom_call" | custom-call | tf_op jit(solution)/shard_map/outer/pallas_call | solution.py:349
  10.0 0.1 collective-permute-start.1
  10.1 1.2 %collective-permute-done.1.theirs_ref = f32[8,256]{1,0:T(8,128)S(1)} collective-permute-done((f32[8,256]{1,0:T(8,128)S(1)}, f32[8,256]{1,0:T(8,128)S(1)}, u32[]{:S(2)}, u32[]{:S(2)}) %collective-permute-start.1) | collective-permute-done | bytes 8224 | tf_op jit(solution)/shard_map/ppermute | solution.py:361
  11.2 0.4 %reduce.1 = (f32[5,8,256]{2,1,0:T(8,128)S(1)}, f32[23,3,8,256]{3,2,1,0:T(8,128)S(1)}) custom-call(f32[24,8,256]{2,1,0:T(8,128)S(1)} %get-tuple-element.22.c_ref, f32[4,8,256]{2,1,0:T(8,128)S(1)} %collective-permute-done.h_ref, f32[8,8,256]{2,1,0:T(8,128)S(1)} %get-tuple-element.26.lap_a, f32[16,8,256]{2,1,0:T(8,128)S(1)} %get-tuple-element.27.lap_b, ...), custom_call_target="tpu_custom_call" | custom-call | tf_op jit(solution)/shard_map/reduce/pallas_call | solution.py:362
  11.6 10.6 %all_to_all.5.all_ref = f32[8,5,8,256]{3,2,1,0:T(8,128)S(1)} all-to-all(f32[8,5,8,256]{3,2,1,0:T(8,128)S(1)} %broadcast_in_dim.2), channel_id=1, replica_groups={{0,2,4,6,8,10,12,14},{16,18,20,22,24,26,28,30},{1,3,5,7,9,11,13,15},{17..., dimensions={0} | all-to-all | bytes 655360 | tf_op jit(solution)/shard_map/all_to_all | solution.py:371
  22.2 1.1 %collective-permute-start.2 = (f32[5,8,256]{2,1,0:T(8,128)S(1)}, f32[5,8,256]{2,1,0:T(8,128)S(1)}, u32[]{:S(2)}, u32[]{:S(2)}) collective-permute-start(f32[5,8,256]{2,1,0:T(8,128)S(1)} %get-tuple-element.35.mine_ref), channel_id=1, source_target_pairs={{0,16},{2,18},{4,20},{6,22},{8,24},{10,26},{12,28},{14,30},{16,0},... | collective-permute-start | bytes 122888 | tf_op jit(solution)/shard_map/ppermute | solution.py:386
  23.3 4.3 %collective-permute-done.2.theirs_ref = f32[5,8,256]{2,1,0:T(8,128)S(1)} collective-permute-done((f32[5,8,256]{2,1,0:T(8,128)S(1)}, f32[5,8,256]{2,1,0:T(8,128)S(1)}, u32[]{:S(2)}, u32[]{:S(2)}) %collective-permute-start.2) | collective-permute-done | bytes 40992 | tf_op jit(solution)/shard_map/ppermute | solution.py:386
  27.6 0.7 %finish.1 = f32[24,8,256]{2,1,0:T(8,128)} custom-call(f32[23,3,8,256]{3,2,1,0:T(8,128)S(1)} %get-tuple-element.33.joint_ref, f32[5,8,256]{2,1,0:T(8,128)S(1)} %get-tuple-element.35.mine_ref, f32[5,8,256]{2,1,0:T(8,128)S(1)} %collective-permute-done.2.theirs_ref, f32[3,8,256]{2,1,0:T(8,128)S(1)} %get-tuple-element.36.refs_0_, ...), custom_call_target="tpu_custom_call" | custom-call | tf_op jit(solution)/shard_map/finish/pallas_call | solution.py:395
  (3 shorter events, 0.1 us)
Async XLA Ops:
  0.8 8.9 %collective-permute-start = (f32[4,8,256]{2,1,0:T(8,128)S(1)}, f32[4,8,256]{2,1,0:T(8,128)S(1)}, u32[]{:S(2)}, u32[]{:S(2)}) collective-permute-start(f32[4,8,256]{2,1,0:T(8,128)S(1)} %pad_maximum_fusion), channel_id=1, source_target_pairs={{0,2},{2,4},{4,6},{6,8},{8,10},{10,12},{12,14},{14,16},{16,18},{18... | collective-permute-start | bytes 98312 | tf_op jit(solution)/shard_map/ppermute | solution.py:326
  10.0 1.2 %collective-permute-start.1 = (f32[8,256]{1,0:T(8,128)S(1)}, f32[8,256]{1,0:T(8,128)S(1)}, u32[]{:S(2)}, u32[]{:S(2)}) collective-permute-start(f32[8,256]{1,0:T(8,128)S(1)} %get-tuple-element.32.mine_ref), channel_id=1, source_target_pairs={{0,1},{1,0},{2,3},{3,2},{4,5},{5,4},{6,7},{7,6},{8,9},{9,8},{10,11... | collective-permute-start | bytes 24584 | tf_op jit(solution)/shard_map/ppermute | solution.py:361
  22.2 5.4 %collective-permute-start.2 = (f32[5,8,256]{2,1,0:T(8,128)S(1)}, f32[5,8,256]{2,1,0:T(8,128)S(1)}, u32[]{:S(2)}, u32[]{:S(2)}) collective-permute-start(f32[5,8,256]{2,1,0:T(8,128)S(1)} %get-tuple-element.35.mine_ref), channel_id=1, source_target_pairs={{0,16},{2,18},{4,20},{6,22},{8,24},{10,26},{12,28},{14,30},{16,0},... | collective-permute-start | bytes 122888 | tf_op jit(solution)/shard_map/ppermute | solution.py:386

commit v5 on v4

--- a/solution.py
+++ b/solution.py
@@ -151,95 +151,91 @@
         ref[n] = jnp.concatenate(blocks[n * per : (n + 1) * per], axis=0).T
 
 
-def inner_kernel(start, v_ref, c_ref, e_ref, lap_ref, joint_ref, edge_ref, far_ref, rs, cs):
+def inner_kernel(v_ref, c_ref, e_ref, lap_ref, joint_ref, edge_ref, far_ref, rs, cs):
     edge_ref[...] = wall_sweep(
-        start, v_ref.shape[0] - 1, v_ref, c_ref, e_ref, None, lap_ref, joint_ref, far_ref, rs, cs
-    )
-
-
-def outer_kernel(
-    stop, v_ref, c_ref, e_ref, h_ref, inner_ref, lap_ref, joint_ref, edge_ref, far_ref, rs, cs
-):
-    edge = wall_sweep(
-        -1, stop, v_ref, c_ref, e_ref, h_ref, lap_ref, joint_ref, far_ref, rs, cs
-    )
-    edge_ref[...] = jnp.concatenate([edge, inner_ref[...]], axis=1)
-
-
-def reduce_kernel(
-    c_ref,
-    h_ref,
-    lap_a,
-    lap_b,
-    wall_a,
-    wall_b,
-    far_a,
-    far_b,
-    mine_ref,
-    theirs_ref,
-    block_ref,
-    joint_ref,
-    ps,
-):
-    rows, planes, width = c_ref.shape
+        1, v_ref.shape[0] - 1, v_ref, c_ref, e_ref, None, lap_ref, joint_ref, far_ref, rs, cs
+    )
+
+
+def outer_kernel(v_ref, c_ref, e_ref, h_ref, lap_ref, joint_ref, edge_ref, far_ref, rs, cs):
+    edge_ref[...] = wall_sweep(
+        -1, 1, v_ref, c_ref, e_ref, h_ref, lap_ref, joint_ref, far_ref, rs, cs
+    )
+
+
+def wall_lines(mine_ref, theirs_ref, wall_ref, far_ref, ps):
+    tiles, width, _ = ps.shape
     seg = width // 8
-    split = far_a.shape[2]
     upper = lax.axis_index("gy") == 1
     s0, r0, c0 = (mine_ref[n : n + 1] for n in range(3))
     s1, r1, c1 = (theirs_ref[n : n + 1] for n in range(3))
     face = 0.5 * normal_rate * (c0 + c1)
     ft = face / (s1 + face)
-    near_all = (r0 + ft * r1) / (s0 + ft * s1)
-    turned = []
-    for at, wall_ref, far_ref in ((0, wall_a, far_a), (split, wall_b, far_b)):
-        lanes = far_ref.shape[2]
-        near = jnp.broadcast_to(near_all[:, at : at + lanes], (8, lanes))
-        far = far_ref[0] + far_ref[1] * near
-        left = jnp.where(upper, near, far)
-        right = jnp.where(upper, far, near)
-        sub = lax.broadcasted_iota(jnp.int32, left.shape, 0)
-
-        def wall_joint(m, wall_ref=wall_ref):
-            return tuple(wall_ref[m - 1, n] for n in range(3))
-
-        for n, h in ((2, 4), (1, 2), (0, 1)):
-            z, ga, gb = wall_joint(seg + n)
-            mid = z + ga * left + gb * right
-            fresh = (sub & h) != 0
-            left, right = (
-                jnp.where(fresh, pltpu.roll(mid, h, 0), left),
-                jnp.where(fresh, pltpu.roll(right, h, 0), mid),
-            )
-
-        def put(m, value, at=at, lanes=lanes):
-            for n in range(lanes // 128):
-                ps[at // 128 + n, pl.ds(m, 8, stride=seg), :] = value[:, n * 128 : n * 128 + 128]
-
-        put(0, left)
-        z, ga, gb = wall_joint(seg - 1)
-        end = z + ga * left + gb * right
-        put(seg - 1, end)
-        tree_down(0, seg - 1, left, end, wall_joint, put)
-        turned += [ps[at // 128 + n].T for n in range(lanes // 128)]
-    first = lap_a.shape[0]
-
-    def visc(i):
-        return h_ref[1] if i < 0 else c_ref[i]
-
+    near = (r0 + ft * r1) / (s0 + ft * s1)
+    near = jnp.broadcast_to(near, mine_ref.shape)
+    far = far_ref[0] + far_ref[1] * near
+    left = jnp.where(upper, near, far)
+    right = jnp.where(upper, far, near)
+    sub = lax.broadcasted_iota(jnp.int32, left.shape, 0)
+
+    def joint(m):
+        return tuple(wall_ref[m - 1, n] for n in range(3))
+
+    for n, h in ((2, 4), (1, 2), (0, 1)):
+        z, ga, gb = joint(seg + n)
+        mid = z + ga * left + gb * right
+        fresh = (sub & h) != 0
+        left, right = (
+            jnp.where(fresh, pltpu.roll(mid, h, 0), left),
+            jnp.where(fresh, pltpu.roll(right, h, 0), mid),
+        )
+
+    def put(m, value):
+        for n in range(tiles):
+            ps[n, pl.ds(m, 8, stride=seg), :] = value[:, n * 128 : n * 128 + 128]
+
+    put(0, left)
+    z, ga, gb = joint(seg - 1)
+    end = z + ga * left + gb * right
+    put(seg - 1, end)
+    tree_down(0, seg - 1, left, end, joint, put)
+    return [ps[n].T for n in range(tiles)]
+
+
+def stream_leaf(first, visc, lines, lap_ref):
     def leaf(r):
-        lap = lap_a[r] if r < first else lap_b[r - first]
-        at = r * planes if r < first else split + (r - first) * planes
-        q = turned[at // 128][at % 128 : at % 128 + planes] - lap
+        planes = lap_ref.shape[1]
+        at = (r - first) * planes
+        q = lines[at // 128][at % 128 : at % 128 + planes] - lap_ref[r - first]
         o = 0.5 * stream_rate * (visc(r - 1) + visc(r))
         return (o, jnp.ones_like(q), None, q, None)
 
-    def keep(m, joint):
-        for n in range(3):
-            joint_ref[m - 1, n] = joint[n]
-
-    whole = tree_up(0, rows, leaf, keep)
-    for n in range(5):
-        block_ref[n] = whole[n]
+    return leaf
+
+
+def store(ref, values):
+    for n, value in enumerate(values):
+        ref[n] = value
+
+
+def inner_reduce_kernel(
+    c_ref, lap_ref, wall_ref, far_ref, mine_ref, theirs_ref, block_ref, joint_ref, ps
+):
+    lines = wall_lines(mine_ref, theirs_ref, wall_ref, far_ref, ps)
+    leaf = stream_leaf(2, lambda i: c_ref[i], lines, lap_ref)
+    block = tree_up(2, c_ref.shape[0], leaf, lambda m, joint: store(joint_ref.at[m - 3], joint))
+    store(block_ref, (block[0], block[1], block[2], block[3], block[4]))
+
+
+def outer_reduce_kernel(
+    c_ref, h_ref, lap_ref, wall_ref, far_ref, mine_ref, theirs_ref, inner_ref, block_ref, joint_ref, ps
+):
+    lines = wall_lines(mine_ref, theirs_ref, wall_ref, far_ref, ps)
+    leaf = stream_leaf(0, lambda i: h_ref[1] if i < 0 else c_ref[i], lines, lap_ref)
+    block = tree_up(0, 2, leaf, lambda m, joint: store(joint_ref.at[m - 1], joint))
+    block, joint = merge(block, tuple(inner_ref[n] for n in range(5)))
+    store(joint_ref.at[1], joint)
+    store(block_ref, block)
 
 
 def join(bit, mine_ref, theirs_ref):
@@ -281,7 +277,7 @@
         joint_ref[n] = joint[n]
 
 
-def finish_kernel(bits, joint_ref, mine_ref, theirs_ref, *refs):
+def finish_kernel(bits, outer_ref, inner_ref, mine_ref, theirs_ref, *refs):
     out_ref = refs[-1]
     rows = out_ref.shape[0]
     right, (_, sl, sr, rl, rr), (z, ga, gb) = join(bits[-1], mine_ref, theirs_ref)
@@ -294,13 +290,17 @@
         low, high = jnp.where(right, mid, low), jnp.where(right, high, mid)
 
     def joint(m):
-        return tuple(joint_ref[m - 1, n] for n in range(3))
+        return tuple(outer_ref[m - 1, n] if m < 3 else inner_ref[m - 3, n] for n in range(3))
 
     def put(m, value):
         out_ref[m - 1] = value
 
     put(rows, high)
-    tree_down(0, rows, low, high, joint, put)
+    z, ga, gb = joint(2)
+    mid = z + ga * low + gb * high
+    put(2, mid)
+    tree_down(0, 2, low, mid, joint, put)
+    tree_down(2, rows, mid, high, joint, put)
 
 
 def per_device(velocity, viscosity, explicit):
@@ -308,9 +308,7 @@
     count = lax.axis_size("gx")
     seg = width // 8
     per = 128 // planes
-    tiles = -(-rows // per)
-    inside = (tiles - 1) * per
-    outside = rows - inside
+    tiles = -(-(rows - 2) // per)
 
     def array(*shape):
         return jax.ShapeDtypeStruct(shape, jnp.float32)
@@ -333,39 +331,43 @@
         cost_estimate=cost(8 << 20),
         name="load",
     )(*(pltpu.with_memory_space_constraint(x, pltpu.HBM) for x in (velocity, viscosity, explicit)))
-    lap_b, wall_b, edge_b, far_b = pl.pallas_call(
-        functools.partial(inner_kernel, outside - 1),
-        out_shape=[
-            array(inside, planes, width),
-            array(seg + 2, 3, 8, (tiles - 1) * 128),
-            array(8, (tiles - 1) * 128),
-            array(2, 8, (tiles - 1) * 128),
-        ],
-        scratch_shapes=[pltpu.VMEM((tiles - 1, width, 128), jnp.float32)] * 2,
+
+    def sweep(kernel, lines, tiles, *args, **more):
+        return pl.pallas_call(
+            kernel,
+            out_shape=[
+                array(lines, planes, width),
+                array(seg + 2, 3, 8, tiles * 128),
+                array(8, tiles * 128),
+                array(2, 8, tiles * 128),
+            ],
+            scratch_shapes=[pltpu.VMEM((tiles, width, 128), jnp.float32)] * 2,
+            compiler_params=params,
+            **more,
+        )(*args)
+
+    def swap(edge):
+        return lax.ppermute(edge, "gy", [(0, 1), (1, 0)])
+
+    lap_b, wall_b, edge_b, far_b = sweep(
+        inner_kernel, rows - 2, tiles, v, c, e, cost_estimate=cost(8 << 20), name="inner"
+    )
+    inner, joints_b = pl.pallas_call(
+        inner_reduce_kernel,
+        out_shape=[block_shape, array(rows - 3, 3, planes, width)],
+        scratch_shapes=[pltpu.VMEM((tiles, width, 128), jnp.float32)],
         compiler_params=params,
         cost_estimate=cost(8 << 20),
-        name="inner",
-    )(v, c, e)
-    lap_a, wall_a, edge, far_a = pl.pallas_call(
-        functools.partial(outer_kernel, outside - 1),
-        out_shape=[
-            array(outside, planes, width),
-            array(seg + 2, 3, 8, 128),
-            array(8, tiles * 128),
-            array(2, 8, 128),
-        ],
-        scratch_shapes=[pltpu.VMEM((1, width, 128), jnp.float32)] * 2,
+        name="inner_reduce",
+    )(c, lap_b, wall_b, far_b, edge_b, swap(edge_b))
+    lap_a, wall_a, edge_a, far_a = sweep(outer_kernel, 2, 1, v, c, e, halo, name="outer")
+    block, joints_a = pl.pallas_call(
+        outer_reduce_kernel,
+        out_shape=[block_shape, array(2, 3, planes, width)],
+        scratch_shapes=[pltpu.VMEM((1, width, 128), jnp.float32)],
         compiler_params=params,
-        name="outer",
-    )(v, c, e, halo, edge_b)
-    other = lax.ppermute(edge, "gy", [(0, 1), (1, 0)])
-    block, joints = pl.pallas_call(
-        reduce_kernel,
-        out_shape=[block_shape, array(rows - 1, 3, planes, width)],
-        scratch_shapes=[pltpu.VMEM((tiles, width, 128), jnp.float32)],
-        compiler_params=params,
-        name="reduce",
-    )(c, halo, lap_a, lap_b, wall_a, wall_b, far_a, far_b, edge, other)
+        name="outer_reduce",
+    )(c, halo, lap_a, wall_a, far_a, edge_a, swap(edge_a), inner)
     bits = [1 << n for n in range(count.bit_length() - 1)]
     group = 1 << min(3, len(bits) - 1)
     everyone = lax.all_to_all(
@@ -397,7 +399,7 @@
         out_shape=field,
         compiler_params=params,
         name="finish",
-    )(joints, block, partner, *path)
+    )(joints_a, joints_b, block, partner, *path)
 
 
 def solution(mesh):

time: 28.6 us -> 28.5 us (level)
  waiting for transfers between devices: 9.91 us -> 9.1 us
  Pallas kernels: 2.94 us -> 3.49 us
    pallas_call x3 -> x4, Pallas kernels: 1.01 us -> 1.56 us  [the longest x2 1.03 us: sweep(): pl.pallas_call(kernel, out_shape=[array(lines, planes, width), array(seg...]
    ppermute x1, waiting for transfers between devices: 4.41 us -> 3.96 us  [per_device(): lax.ppermute(message, 'gx', [(i, (i + 1) % count) for i in range(count)])]
    ppermute x1 -> x2, waiting for transfers between devices: 1.16 us -> 0.79 us  [swap(): return lax.ppermute(edge, 'gy', [(0, 1), (1, 0)])]
  transfers between devices with their start and end apart: 3 -> 4, of which waited for: 3 -> 3; matrix products, arithmetic and copies ran while one was open for 0% -> 0% of each run, Pallas kernels for 5% -> 9%
where the time goes in v5:
time: 28.5 us; the launch traced here: 28.2 us
  blocking collectives  10.6 us (37%)
  waiting for transfers between devices  9.1 us (32%)
  starting transfers between devices  4.19 us (15%)
  Pallas kernels  3.49 us (12%)
  other arithmetic  0.77 us (3%)
    all_to_all x1, blocking collectives, per_device(): lax.all_to_all(jnp.broadcast_to(block[None], (group,) + block.shape), 'gx...  10.6 us
    ppermute x1, waiting for transfers between devices, per_device(): partner = lax.ppermute(block, 'gx', [(i, i ^ bit) for i in range(count)])  4.35 us
    ppermute x1, waiting for transfers between devices, per_device(): lax.ppermute(message, 'gx', [(i, (i + 1) % count) for i in range(count)])  3.96 us
    ppermute x1, starting transfers between devices, per_device(): lax.ppermute(message, 'gx', [(i, (i + 1) % count) for i in range(count)])  2.99 us
    pallas_call x1, Pallas kernels, per_device(): pl.pallas_call(load_kernel, out_shape=[field] * 3, in_specs=[pl.BlockSpec...  1.14 us
    ppermute x1, starting transfers between devices, per_device(): partner = lax.ppermute(block, 'gx', [(i, i ^ bit) for i in range(count)])  1.06 us
    pallas_call x2, Pallas kernels, sweep(): pl.pallas_call(kernel, out_shape=[array(lines, planes, width), array(seg...  1.03 us
    ppermute x2, waiting for transfers between devices, swap(): return lax.ppermute(edge, 'gy', [(0, 1), (1, 0)])  0.79 us
  transfers between devices with their start and end apart: 4, of which 3 were waited for; matrix products, arithmetic and copies ran while one was open for 0% of the time, Pallas kernels for 9%

profile of v5, /device:TPU:0, one launch (start us, length us, event | category | flops | bytes accessed | tf_op | source)
XLA Modules:
  0.0 28.2 jit_solution(12059394774902620741)
XLA Ops:
  0.0 0.8 %add_subtract_fusion = (f32[1,8,256]{2,1,0:T(8,128)S(1)}, f32[1,8,256]{2,1,0:T(8,128)S(1)}, f32[1,8,256]{2,1,0:T(8,128)S(1)}, f32[1,8,256]{2,1,0:T(8,128)S(1)}) fusion(f32[24,8,256]{2,1,0:T(8,128)} %e_hbm.1, f32[24,8,256]{2,1,0:T(8,128)} %v_hbm.1, f32[24,8,256]{2,1,0:T(8,128)} %c_hbm.1), kind=kLoop, calls=%fused_computation.1 | loop fusion | flops 12288 | bytes 73728 | tf_op jit(solution)/shard_map/sub | solution.py:323
  0.8 3.0 %collective-permute-start = (f32[4,8,256]{2,1,0:T(8,128)S(1)}, f32[4,8,256]{2,1,0:T(8,128)S(1)}, u32[]{:S(2)}, u32[]{:S(2)}) collective-permute-start(f32[4,8,256]{2,1,0:T(8,128)S(1)} %pad_maximum_fusion), channel_id=1, source_target_pairs={{0,2},{2,4},{4,6},{6,8},{8,10},{10,12},{12,14},{14,16},{16,18},{18... | collective-permute-start | bytes 98312 | tf_op jit(solution)/shard_map/ppermute | solution.py:324
  3.8 1.1 %load.1 = (f32[24,8,256]{2,1,0:T(8,128)S(1)}, f32[24,8,256]{2,1,0:T(8,128)S(1)}, f32[24,8,256]{2,1,0:T(8,128)S(1)}) custom-call(f32[24,8,256]{2,1,0:T(8,128)} %v_hbm.1, f32[24,8,256]{2,1,0:T(8,128)} %c_hbm.1, f32[24,8,256]{2,1,0:T(8,128)} %e_hbm.1), custom_call_target="tpu_custom_call" | custom-call | bytes 8388608 | tf_op jit(solution)/shard_map/load/pallas_call | solution.py:325
  4.9 0.7 %inner.1 = (f32[22,8,256]{2,1,0:T(8,128)S(1)}, f32[34,3,8,256]{3,2,1,0:T(8,128)S(1)}, f32[8,256]{1,0:T(8,128)S(1)}, f32[2,8,256]{2,1,0:T(8,128)S(1)}) custom-call(f32[24,8,256]{2,1,0:T(8,128)S(1)} %get-tuple-element.25.v_ref, f32[24,8,256]{2,1,0:T(8,128)S(1)} %get-tuple-element.24.c_ref, f32[24,8,256]{2,1,0:T(8,128)S(1)} %get-tuple-element.26.e_ref), custom_call_target="tpu_custom_call" | custom-call | bytes 8388608 | tf_op jit(solution)/shard_map/inner/pallas_call | solution.py:336
  5.6 0.1 collective-permute-start.2
  5.7 4.0 %collective-permute-done.h_ref = f32[4,8,256]{2,1,0:T(8,128)S(1)} collective-permute-done((f32[4,8,256]{2,1,0:T(8,128)S(1)}, f32[4,8,256]{2,1,0:T(8,128)S(1)}, u32[]{:S(2)}, u32[]{:S(2)}) %collective-permute-start) | collective-permute-done | bytes 32800 | tf_op jit(solution)/shard_map/ppermute | solution.py:324
  9.7 0.3 %outer.1 = (f32[2,8,256]{2,1,0:T(8,128)S(1)}, f32[34,3,8,128]{3,2,1,0:T(8,128)S(1)}, f32[8,128]{1,0:T(8,128)S(1)}, f32[2,8,128]{2,1,0:T(8,128)S(1)}) custom-call(f32[24,8,256]{2,1,0:T(8,128)S(1)} %get-tuple-element.25.v_ref, f32[24,8,256]{2,1,0:T(8,128)S(1)} %get-tuple-element.24.c_ref, f32[24,8,256]{2,1,0:T(8,128)S(1)} %get-tuple-element.26.e_ref, ...), custom_call_target="tpu_custom_call" | custom-call | tf_op jit(solution)/shard_map/outer/pallas_call | solution.py:336
  10.0 0.1 collective-permute-start.1
  10.1 0.0 collective-permute-done.2.theirs_ref
  10.1 0.3 %inner_reduce.1 = (f32[5,8,256]{2,1,0:T(8,128)S(1)}, f32[21,3,8,256]{3,2,1,0:T(8,128)S(1)}) custom-call(f32[24,8,256]{2,1,0:T(8,128)S(1)} %get-tuple-element.24.c_ref, f32[22,8,256]{2,1,0:T(8,128)S(1)} %get-tuple-element.31.lap_ref, f32[34,3,8,256]{3,2,1,0:T(8,128)S(1)} %get-tuple-element.32.wall_ref, f32[2,8,256]{2,1,0:T(8,128)S(1)} %get-tuple-element.33.far_ref, ...), custom_call_target="tpu_custom_call" | custom-call | bytes 8388608 | tf_op jit(solution)/shard_map/inner_reduce/pallas_call | solution.py:355
  10.4 0.8 %collective-permute-done.1.theirs_ref = f32[8,128]{1,0:T(8,128)S(1)} collective-permute-done((f32[8,128]{1,0:T(8,128)S(1)}, f32[8,128]{1,0:T(8,128)S(1)}, u32[]{:S(2)}, u32[]{:S(2)}) %collective-permute-start.1) | collective-permute-done | bytes 4128 | tf_op jit(solution)/shard_map/ppermute | solution.py:350
  11.2 0.2 outer_reduce.1
  11.4 10.6 %all_to_all.5.all_ref = f32[8,5,8,256]{3,2,1,0:T(8,128)S(1)} all-to-all(f32[8,5,8,256]{3,2,1,0:T(8,128)S(1)} %broadcast_in_dim.2), channel_id=1, replica_groups={{0,2,4,6,8,10,12,14},{16,18,20,22,24,26,28,30},{1,3,5,7,9,11,13,15},{17..., dimensions={0} | all-to-all | bytes 655360 | tf_op jit(solution)/shard_map/all_to_all | solution.py:373
  22.1 1.1 %collective-permute-start.3 = (f32[5,8,256]{2,1,0:T(8,128)S(1)}, f32[5,8,256]{2,1,0:T(8,128)S(1)}, u32[]{:S(2)}, u32[]{:S(2)}) collective-permute-start(f32[5,8,256]{2,1,0:T(8,128)S(1)} %get-tuple-element.39.mine_ref), channel_id=1, source_target_pairs={{0,16},{2,18},{4,20},{6,22},{8,24},{10,26},{12,28},{14,30},{16,0},... | collective-permute-start | bytes 122888 | tf_op jit(solution)/shard_map/ppermute | solution.py:388
  23.1 4.3 %collective-permute-done.3.theirs_ref = f32[5,8,256]{2,1,0:T(8,128)S(1)} collective-permute-done((f32[5,8,256]{2,1,0:T(8,128)S(1)}, f32[5,8,256]{2,1,0:T(8,128)S(1)}, u32[]{:S(2)}, u32[]{:S(2)}) %collective-permute-start.3) | collective-permute-done | bytes 40992 | tf_op jit(solution)/shard_map/ppermute | solution.py:388
  27.5 0.7 %finish.1 = f32[24,8,256]{2,1,0:T(8,128)} custom-call(f32[2,3,8,256]{3,2,1,0:T(8,128)S(1)} %get-tuple-element.36.outer_ref, f32[21,3,8,256]{3,2,1,0:T(8,128)S(1)} %get-tuple-element.37.inner_ref, f32[5,8,256]{2,1,0:T(8,128)S(1)} %get-tuple-element.39.mine_ref, f32[5,8,256]{2,1,0:T(8,128)S(1)} %collective-permute-done.3.theirs_ref, ...), custom_call_target="tpu_custom_call" | custom-call | tf_op jit(solution)/shard_map/finish/pallas_call | solution.py:397
  (3 shorter events, 0.1 us)
Async XLA Ops:
  0.8 8.9 %collective-permute-start = (f32[4,8,256]{2,1,0:T(8,128)S(1)}, f32[4,8,256]{2,1,0:T(8,128)S(1)}, u32[]{:S(2)}, u32[]{:S(2)}) collective-permute-start(f32[4,8,256]{2,1,0:T(8,128)S(1)} %pad_maximum_fusion), channel_id=1, source_target_pairs={{0,2},{2,4},{4,6},{6,8},{8,10},{10,12},{12,14},{14,16},{16,18},{18... | collective-permute-start | bytes 98312 | tf_op jit(solution)/shard_map/ppermute | solution.py:324
  5.6 4.5 %collective-permute-start.2 = (f32[8,256]{1,0:T(8,128)S(1)}, f32[8,256]{1,0:T(8,128)S(1)}, u32[]{:S(2)}, u32[]{:S(2)}) collective-permute-start(f32[8,256]{1,0:T(8,128)S(1)} %get-tuple-element.34.mine_ref), channel_id=1, source_target_pairs={{0,1},{1,0},{2,3},{3,2},{4,5},{5,4},{6,7},{7,6},{8,9},{9,8},{10,11... | collective-permute-start | bytes 24584 | tf_op jit(solution)/shard_map/ppermute | solution.py:350
  10.0 1.2 %collective-permute-start.1 = (f32[8,128]{1,0:T(8,128)S(1)}, f32[8,128]{1,0:T(8,128)S(1)}, u32[]{:S(2)}, u32[]{:S(2)}) collective-permute-start(f32[8,128]{1,0:T(8,128)S(1)} %get-tuple-element.30.mine_ref), channel_id=1, source_target_pairs={{0,1},{1,0},{2,3},{3,2},{4,5},{5,4},{6,7},{7,6},{8,9},{9,8},{10,11... | collective-permute-start | bytes 12296 | tf_op jit(solution)/shard_map/ppermute | solution.py:350
  22.1 5.4 %collective-permute-start.3 = (f32[5,8,256]{2,1,0:T(8,128)S(1)}, f32[5,8,256]{2,1,0:T(8,128)S(1)}, u32[]{:S(2)}, u32[]{:S(2)}) collective-permute-start(f32[5,8,256]{2,1,0:T(8,128)S(1)} %get-tuple-element.39.mine_ref), channel_id=1, source_target_pairs={{0,16},{2,18},{4,20},{6,22},{8,24},{10,26},{12,28},{14,30},{16,0},... | collective-permute-start | bytes 122888 | tf_op jit(solution)/shard_map/ppermute | solution.py:388

commit v6 on v5

--- a/solution.py
+++ b/solution.py
@@ -249,7 +249,7 @@
 
 
 def group_kernel(all_ref, block_ref, *joint_refs):
-    blocks = [tuple(all_ref[m, n] for n in range(5)) for m in range(all_ref.shape[0])]
+    blocks = [tuple(all_ref[m, n] for n in range(5)) for m in reversed(range(all_ref.shape[0]))]
     place = lax.axis_index("gx") & (len(blocks) - 1)
     for level, ref in enumerate(joint_refs):
         merged = [merge(blocks[m], blocks[m + 1]) for m in range(0, len(blocks), 2)]
@@ -376,7 +376,7 @@
         0,
         0,
         tiled=True,
-        axis_index_groups=[list(range(i, i + group)) for i in range(0, count, group)],
+        axis_index_groups=[list(range(i, i + group))[::-1] for i in range(0, count, group)],
     )
     block, *path = pl.pallas_call(
         group_kernel,

time: 28.5 us -> 27.1 us (0.951)
  blocking collectives: 10.6 us -> 9.63 us
  waiting for transfers between devices: 9.1 us -> 8.62 us
    all_to_all x1, blocking collectives: 10.6 us -> 9.63 us  [per_device(): lax.all_to_all(jnp.broadcast_to(block[None], (group,) + block.shape), 'gx...]
    ppermute x1, waiting for transfers between devices: 4.35 us -> 3.86 us  [per_device(): partner = lax.ppermute(block, 'gx', [(i, i ^ bit) for i in range(count)])]
where the time goes in v6:
time: 27.1 us; the launch traced here: 26.8 us
  blocking collectives  9.63 us (36%)
  waiting for transfers between devices  8.62 us (32%)
  starting transfers between devices  4.23 us (16%)
  Pallas kernels  3.49 us (13%)
  other arithmetic  0.77 us (3%)
    all_to_all x1, blocking collectives, per_device(): lax.all_to_all(jnp.broadcast_to(block[None], (group,) + block.shape), 'gx...  9.63 us
    ppermute x1, waiting for transfers between devices, per_device(): lax.ppermute(message, 'gx', [(i, (i + 1) % count) for i in range(count)])  3.96 us
    ppermute x1, waiting for transfers between devices, per_device(): partner = lax.ppermute(block, 'gx', [(i, i ^ bit) for i in range(count)])  3.86 us
    ppermute x1, starting transfers between devices, per_device(): lax.ppermute(message, 'gx', [(i, (i + 1) % count) for i in range(count)])  2.99 us
    pallas_call x1, Pallas kernels, per_device(): pl.pallas_call(load_kernel, out_shape=[field] * 3, in_specs=[pl.BlockSpec...  1.14 us
    ppermute x1, starting transfers between devices, per_device(): partner = lax.ppermute(block, 'gx', [(i, i ^ bit) for i in range(count)])  1.1 us
    pallas_call x2, Pallas kernels, sweep(): pl.pallas_call(kernel, out_shape=[array(lines, planes, width), array(seg...  1.03 us
    ppermute x2, waiting for transfers between devices, swap(): return lax.ppermute(edge, 'gy', [(0, 1), (1, 0)])  0.79 us
  transfers between devices with their start and end apart: 4, of which 3 were waited for; matrix products, arithmetic and copies ran while one was open for 0% of the time, Pallas kernels for 9%

profile of v6, /device:TPU:0, one launch (start us, length us, event | category | flops | bytes accessed | tf_op | source)
XLA Modules:
  0.0 26.8 jit_solution(5737070959354983301)
XLA Ops:
  0.0 0.8 %add_subtract_fusion = (f32[1,8,256]{2,1,0:T(8,128)S(1)}, f32[1,8,256]{2,1,0:T(8,128)S(1)}, f32[1,8,256]{2,1,0:T(8,128)S(1)}, f32[1,8,256]{2,1,0:T(8,128)S(1)}) fusion(f32[24,8,256]{2,1,0:T(8,128)} %e_hbm.1, f32[24,8,256]{2,1,0:T(8,128)} %v_hbm.1, f32[24,8,256]{2,1,0:T(8,128)} %c_hbm.1), kind=kLoop, calls=%fused_computation.1 | loop fusion | flops 12288 | bytes 73728 | tf_op jit(solution)/shard_map/sub | solution.py:323
  0.8 3.0 %collective-permute-start = (f32[4,8,256]{2,1,0:T(8,128)S(1)}, f32[4,8,256]{2,1,0:T(8,128)S(1)}, u32[]{:S(2)}, u32[]{:S(2)}) collective-permute-start(f32[4,8,256]{2,1,0:T(8,128)S(1)} %pad_maximum_fusion), channel_id=1, source_target_pairs={{0,2},{2,4},{4,6},{6,8},{8,10},{10,12},{12,14},{14,16},{16,18},{18... | collective-permute-start | bytes 98312 | tf_op jit(solution)/shard_map/ppermute | solution.py:324
  3.8 1.1 %load.1 = (f32[24,8,256]{2,1,0:T(8,128)S(1)}, f32[24,8,256]{2,1,0:T(8,128)S(1)}, f32[24,8,256]{2,1,0:T(8,128)S(1)}) custom-call(f32[24,8,256]{2,1,0:T(8,128)} %v_hbm.1, f32[24,8,256]{2,1,0:T(8,128)} %c_hbm.1, f32[24,8,256]{2,1,0:T(8,128)} %e_hbm.1), custom_call_target="tpu_custom_call" | custom-call | bytes 8388608 | tf_op jit(solution)/shard_map/load/pallas_call | solution.py:325
  4.9 0.7 %inner.1 = (f32[22,8,256]{2,1,0:T(8,128)S(1)}, f32[34,3,8,256]{3,2,1,0:T(8,128)S(1)}, f32[8,256]{1,0:T(8,128)S(1)}, f32[2,8,256]{2,1,0:T(8,128)S(1)}) custom-call(f32[24,8,256]{2,1,0:T(8,128)S(1)} %get-tuple-element.25.v_ref, f32[24,8,256]{2,1,0:T(8,128)S(1)} %get-tuple-element.24.c_ref, f32[24,8,256]{2,1,0:T(8,128)S(1)} %get-tuple-element.26.e_ref), custom_call_target="tpu_custom_call" | custom-call | bytes 8388608 | tf_op jit(solution)/shard_map/inner/pallas_call | solution.py:336
  5.6 0.1 collective-permute-start.2
  5.7 4.0 %collective-permute-done.h_ref = f32[4,8,256]{2,1,0:T(8,128)S(1)} collective-permute-done((f32[4,8,256]{2,1,0:T(8,128)S(1)}, f32[4,8,256]{2,1,0:T(8,128)S(1)}, u32[]{:S(2)}, u32[]{:S(2)}) %collective-permute-start) | collective-permute-done | bytes 32800 | tf_op jit(solution)/shard_map/ppermute | solution.py:324
  9.7 0.3 %outer.1 = (f32[2,8,256]{2,1,0:T(8,128)S(1)}, f32[34,3,8,128]{3,2,1,0:T(8,128)S(1)}, f32[8,128]{1,0:T(8,128)S(1)}, f32[2,8,128]{2,1,0:T(8,128)S(1)}) custom-call(f32[24,8,256]{2,1,0:T(8,128)S(1)} %get-tuple-element.25.v_ref, f32[24,8,256]{2,1,0:T(8,128)S(1)} %get-tuple-element.24.c_ref, f32[24,8,256]{2,1,0:T(8,128)S(1)} %get-tuple-element.26.e_ref, ...), custom_call_target="tpu_custom_call" | custom-call | tf_op jit(solution)/shard_map/outer/pallas_call | solution.py:336
  10.0 0.1 collective-permute-start.1
  10.1 0.0 collective-permute-done.2.theirs_ref
  10.1 0.3 %inner_reduce.1 = (f32[5,8,256]{2,1,0:T(8,128)S(1)}, f32[21,3,8,256]{3,2,1,0:T(8,128)S(1)}) custom-call(f32[24,8,256]{2,1,0:T(8,128)S(1)} %get-tuple-element.24.c_ref, f32[22,8,256]{2,1,0:T(8,128)S(1)} %get-tuple-element.31.lap_ref, f32[34,3,8,256]{3,2,1,0:T(8,128)S(1)} %get-tuple-element.32.wall_ref, f32[2,8,256]{2,1,0:T(8,128)S(1)} %get-tuple-element.33.far_ref, ...), custom_call_target="tpu_custom_call" | custom-call | bytes 8388608 | tf_op jit(solution)/shard_map/inner_reduce/pallas_call | solution.py:355
  10.4 0.8 %collective-permute-done.1.theirs_ref = f32[8,128]{1,0:T(8,128)S(1)} collective-permute-done((f32[8,128]{1,0:T(8,128)S(1)}, f32[8,128]{1,0:T(8,128)S(1)}, u32[]{:S(2)}, u32[]{:S(2)}) %collective-permute-start.1) | collective-permute-done | bytes 4128 | tf_op jit(solution)/shard_map/ppermute | solution.py:350
  11.2 0.2 outer_reduce.1
  11.4 9.6 %all_to_all.5.all_ref = f32[8,5,8,256]{3,2,1,0:T(8,128)S(1)} all-to-all(f32[8,5,8,256]{3,2,1,0:T(8,128)S(1)} %broadcast_in_dim.2), channel_id=1, replica_groups={{14,12,10,8,6,4,2,0},{30,28,26,24,22,20,18,16},{15,13,11,9,7,5,3,1},{31..., dimensions={0} | all-to-all | bytes 655360 | tf_op jit(solution)/shard_map/all_to_all | solution.py:373
  21.1 1.1 %collective-permute-start.3 = (f32[5,8,256]{2,1,0:T(8,128)S(1)}, f32[5,8,256]{2,1,0:T(8,128)S(1)}, u32[]{:S(2)}, u32[]{:S(2)}) collective-permute-start(f32[5,8,256]{2,1,0:T(8,128)S(1)} %get-tuple-element.39.mine_ref), channel_id=1, source_target_pairs={{0,16},{2,18},{4,20},{6,22},{8,24},{10,26},{12,28},{14,30},{16,0},... | collective-permute-start | bytes 122888 | tf_op jit(solution)/shard_map/ppermute | solution.py:388
  22.2 3.9 %collective-permute-done.3.theirs_ref = f32[5,8,256]{2,1,0:T(8,128)S(1)} collective-permute-done((f32[5,8,256]{2,1,0:T(8,128)S(1)}, f32[5,8,256]{2,1,0:T(8,128)S(1)}, u32[]{:S(2)}, u32[]{:S(2)}) %collective-permute-start.3) | collective-permute-done | bytes 40992 | tf_op jit(solution)/shard_map/ppermute | solution.py:388
  26.1 0.7 %finish.1 = f32[24,8,256]{2,1,0:T(8,128)} custom-call(f32[2,3,8,256]{3,2,1,0:T(8,128)S(1)} %get-tuple-element.36.outer_ref, f32[21,3,8,256]{3,2,1,0:T(8,128)S(1)} %get-tuple-element.37.inner_ref, f32[5,8,256]{2,1,0:T(8,128)S(1)} %get-tuple-element.39.mine_ref, f32[5,8,256]{2,1,0:T(8,128)S(1)} %collective-permute-done.3.theirs_ref, ...), custom_call_target="tpu_custom_call" | custom-call | tf_op jit(solution)/shard_map/finish/pallas_call | solution.py:397
  (3 shorter events, 0.1 us)
Async XLA Ops:
  0.8 8.9 %collective-permute-start = (f32[4,8,256]{2,1,0:T(8,128)S(1)}, f32[4,8,256]{2,1,0:T(8,128)S(1)}, u32[]{:S(2)}, u32[]{:S(2)}) collective-permute-start(f32[4,8,256]{2,1,0:T(8,128)S(1)} %pad_maximum_fusion), channel_id=1, source_target_pairs={{0,2},{2,4},{4,6},{6,8},{8,10},{10,12},{12,14},{14,16},{16,18},{18... | collective-permute-start | bytes 98312 | tf_op jit(solution)/shard_map/ppermute | solution.py:324
  5.6 4.5 %collective-permute-start.2 = (f32[8,256]{1,0:T(8,128)S(1)}, f32[8,256]{1,0:T(8,128)S(1)}, u32[]{:S(2)}, u32[]{:S(2)}) collective-permute-start(f32[8,256]{1,0:T(8,128)S(1)} %get-tuple-element.34.mine_ref), channel_id=1, source_target_pairs={{0,1},{1,0},{2,3},{3,2},{4,5},{5,4},{6,7},{7,6},{8,9},{9,8},{10,11... | collective-permute-start | bytes 24584 | tf_op jit(solution)/shard_map/ppermute | solution.py:350
  10.0 1.2 %collective-permute-start.1 = (f32[8,128]{1,0:T(8,128)S(1)}, f32[8,128]{1,0:T(8,128)S(1)}, u32[]{:S(2)}, u32[]{:S(2)}) collective-permute-start(f32[8,128]{1,0:T(8,128)S(1)} %get-tuple-element.30.mine_ref), channel_id=1, source_target_pairs={{0,1},{1,0},{2,3},{3,2},{4,5},{5,4},{6,7},{7,6},{8,9},{9,8},{10,11... | collective-permute-start | bytes 12296 | tf_op jit(solution)/shard_map/ppermute | solution.py:350
  21.1 5.0 %collective-permute-start.3 = (f32[5,8,256]{2,1,0:T(8,128)S(1)}, f32[5,8,256]{2,1,0:T(8,128)S(1)}, u32[]{:S(2)}, u32[]{:S(2)}) collective-permute-start(f32[5,8,256]{2,1,0:T(8,128)S(1)} %get-tuple-element.39.mine_ref), channel_id=1, source_target_pairs={{0,16},{2,18},{4,20},{6,22},{8,24},{10,26},{12,28},{14,30},{16,0},... | collective-permute-start | bytes 122888 | tf_op jit(solution)/shard_map/ppermute | solution.py:388

commit v7 on v6

--- a/solution.py
+++ b/solution.py
@@ -9,6 +9,7 @@
 
 stream_rate = 1000.0
 normal_rate = 50.0
+pad = 1
 params = pltpu.CompilerParams(vmem_limit_bytes=8 << 20)
 
 
@@ -97,7 +98,7 @@
 
     def load(ref, m):
         return jnp.concatenate(
-            [ref[n, pl.ds(m, 8, stride=seg), :] for n in range(ref.shape[0])], axis=1
+            [ref[n, pl.ds(m, 8, stride=seg + pad), :] for n in range(ref.shape[0])], axis=1
         )
 
     sub = lax.broadcasted_iota(jnp.int32, (8, rs.shape[0] * 128), 0)
@@ -146,9 +147,12 @@
 
 
 def turn(blocks, ref):
+    seg = blocks[0].shape[1] // 8
     per = 128 // blocks[0].shape[0]
     for n in range(ref.shape[0]):
-        ref[n] = jnp.concatenate(blocks[n * per : (n + 1) * per], axis=0).T
+        lines = jnp.concatenate(blocks[n * per : (n + 1) * per], axis=0).T
+        for k in range(8):
+            ref[n, pl.ds(k * (seg + pad), seg), :] = lines[k * seg : (k + 1) * seg]
 
 
 def inner_kernel(v_ref, c_ref, e_ref, lap_ref, joint_ref, edge_ref, far_ref, rs, cs):
@@ -164,8 +168,8 @@
 
 
 def wall_lines(mine_ref, theirs_ref, wall_ref, far_ref, ps):
-    tiles, width, _ = ps.shape
-    seg = width // 8
+    tiles = ps.shape[0]
+    seg = ps.shape[1] // 8 - pad
     upper = lax.axis_index("gy") == 1
     s0, r0, c0 = (mine_ref[n : n + 1] for n in range(3))
     s1, r1, c1 = (theirs_ref[n : n + 1] for n in range(3))
@@ -192,14 +196,15 @@
 
     def put(m, value):
         for n in range(tiles):
-            ps[n, pl.ds(m, 8, stride=seg), :] = value[:, n * 128 : n * 128 + 128]
+            ps[n, pl.ds(m, 8, stride=seg + pad), :] = value[:, n * 128 : n * 128 + 128]
 
     put(0, left)
     z, ga, gb = joint(seg - 1)
     end = z + ga * left + gb * right
     put(seg - 1, end)
     tree_down(0, seg - 1, left, end, joint, put)
-    return [ps[n].T for n in range(tiles)]
+    pieces = [pl.ds(k * (seg + pad), seg) for k in range(8)]
+    return [jnp.concatenate([ps[n, piece, :] for piece in pieces], axis=0).T for n in range(tiles)]
 
 
 def stream_leaf(first, visc, lines, lap_ref):
@@ -341,7 +346,7 @@
                 array(8, tiles * 128),
                 array(2, 8, tiles * 128),
             ],
-            scratch_shapes=[pltpu.VMEM((tiles, width, 128), jnp.float32)] * 2,
+            scratch_shapes=[pltpu.VMEM((tiles, width + 8 * pad, 128), jnp.float32)] * 2,
             compiler_params=params,
             **more,
         )(*args)
@@ -355,7 +360,7 @@
     inner, joints_b = pl.pallas_call(
         inner_reduce_kernel,
         out_shape=[block_shape, array(rows - 3, 3, planes, width)],
-        scratch_shapes=[pltpu.VMEM((tiles, width, 128), jnp.float32)],
+        scratch_shapes=[pltpu.VMEM((tiles, width + 8 * pad, 128), jnp.float32)],
         compiler_params=params,
         cost_estimate=cost(8 << 20),
         name="inner_reduce",
@@ -364,7 +369,7 @@
     block, joints_a = pl.pallas_call(
         outer_reduce_kernel,
         out_shape=[block_shape, array(2, 3, planes, width)],
-        scratch_shapes=[pltpu.VMEM((1, width, 128), jnp.float32)],
+        scratch_shapes=[pltpu.VMEM((1, width + 8 * pad, 128), jnp.float32)],
         compiler_params=params,
         name="outer_reduce",
     )(c, halo, lap_a, wall_a, far_a, edge_a, swap(edge_a), inner)

time: 27.1 us -> 27 us (level)
  Pallas kernels: 3.49 us -> 2.83 us
  waiting for transfers between devices: 8.62 us -> 9.13 us
    pallas_call x2, Pallas kernels: 1.03 us -> 0.55 us  [sweep(): pl.pallas_call(kernel, out_shape=[array(lines, planes, width), array(seg...]
    ppermute x1, waiting for transfers between devices: 3.96 us -> 4.35 us  [per_device(): lax.ppermute(message, 'gx', [(i, (i + 1) % count) for i in range(count)])]
  transfers between devices with their start and end apart: 4 -> 4, of which waited for: 3 -> 3; matrix products, arithmetic and copies ran while one was open for 0% -> 0% of each run, Pallas kernels for 9% -> 7%
where the time goes in v7:
time: 27 us; the launch traced here: 26.7 us
  blocking collectives  9.63 us (36%)
  waiting for transfers between devices  9.13 us (34%)
  starting transfers between devices  4.23 us (16%)
  Pallas kernels  2.83 us (10%)
  other arithmetic  0.77 us (3%)
    all_to_all x1, blocking collectives, per_device(): lax.all_to_all(jnp.broadcast_to(block[None], (group,) + block.shape), 'gx...  9.63 us
    ppermute x1, waiting for transfers between devices, per_device(): lax.ppermute(message, 'gx', [(i, (i + 1) % count) for i in range(count)])  4.35 us
    ppermute x1, waiting for transfers between devices, per_device(): partner = lax.ppermute(block, 'gx', [(i, i ^ bit) for i in range(count)])  3.86 us
    ppermute x1, starting transfers between devices, per_device(): lax.ppermute(message, 'gx', [(i, (i + 1) % count) for i in range(count)])  2.99 us
    pallas_call x1, Pallas kernels, per_device(): pl.pallas_call(load_kernel, out_shape=[field] * 3, in_specs=[pl.BlockSpec...  1.14 us
    ppermute x1, starting transfers between devices, per_device(): partner = lax.ppermute(block, 'gx', [(i, i ^ bit) for i in range(count)])  1.1 us
    ppermute x2, waiting for transfers between devices, swap(): return lax.ppermute(edge, 'gy', [(0, 1), (1, 0)])  0.92 us
    sub x1, other arithmetic, per_device(): message = jnp.stack([tail_v[1], tail_c[1], flux, tail_v[1] + tail_e - flux])  0.77 us
  transfers between devices with their start and end apart: 4, of which 3 were waited for; matrix products, arithmetic and copies ran while one was open for 0% of the time, Pallas kernels for 7%

profile of v7, /device:TPU:0, one launch (start us, length us, event | category | flops | bytes accessed | tf_op | source)
XLA Modules:
  0.0 26.7 jit_solution(11975303782124531995)
XLA Ops:
  0.0 0.8 %add_subtract_fusion = (f32[1,8,256]{2,1,0:T(8,128)S(1)}, f32[1,8,256]{2,1,0:T(8,128)S(1)}, f32[1,8,256]{2,1,0:T(8,128)S(1)}, f32[1,8,256]{2,1,0:T(8,128)S(1)}) fusion(f32[24,8,256]{2,1,0:T(8,128)} %e_hbm.1, f32[24,8,256]{2,1,0:T(8,128)} %v_hbm.1, f32[24,8,256]{2,1,0:T(8,128)} %c_hbm.1), kind=kLoop, calls=%fused_computation.1 | loop fusion | flops 12288 | bytes 73728 | tf_op jit(solution)/shard_map/sub | solution.py:328
  0.8 3.0 %collective-permute-start = (f32[4,8,256]{2,1,0:T(8,128)S(1)}, f32[4,8,256]{2,1,0:T(8,128)S(1)}, u32[]{:S(2)}, u32[]{:S(2)}) collective-permute-start(f32[4,8,256]{2,1,0:T(8,128)S(1)} %pad_maximum_fusion), channel_id=1, source_target_pairs={{0,2},{2,4},{4,6},{6,8},{8,10},{10,12},{12,14},{14,16},{16,18},{18... | collective-permute-start | bytes 98312 | tf_op jit(solution)/shard_map/ppermute | solution.py:329
  3.8 1.1 %load.1 = (f32[24,8,256]{2,1,0:T(8,128)S(1)}, f32[24,8,256]{2,1,0:T(8,128)S(1)}, f32[24,8,256]{2,1,0:T(8,128)S(1)}) custom-call(f32[24,8,256]{2,1,0:T(8,128)} %v_hbm.1, f32[24,8,256]{2,1,0:T(8,128)} %c_hbm.1, f32[24,8,256]{2,1,0:T(8,128)} %e_hbm.1), custom_call_target="tpu_custom_call" | custom-call | bytes 8388608 | tf_op jit(solution)/shard_map/load/pallas_call | solution.py:330
  4.9 0.3 %inner.1 = (f32[22,8,256]{2,1,0:T(8,128)S(1)}, f32[34,3,8,256]{3,2,1,0:T(8,128)S(1)}, f32[8,256]{1,0:T(8,128)S(1)}, f32[2,8,256]{2,1,0:T(8,128)S(1)}) custom-call(f32[24,8,256]{2,1,0:T(8,128)S(1)} %get-tuple-element.25.v_ref, f32[24,8,256]{2,1,0:T(8,128)S(1)} %get-tuple-element.24.c_ref, f32[24,8,256]{2,1,0:T(8,128)S(1)} %get-tuple-element.26.e_ref), custom_call_target="tpu_custom_call" | custom-call | bytes 8388608 | tf_op jit(solution)/shard_map/inner/pallas_call | solution.py:341
  5.2 0.1 collective-permute-start.2
  5.3 4.3 %collective-permute-done.h_ref = f32[4,8,256]{2,1,0:T(8,128)S(1)} collective-permute-done((f32[4,8,256]{2,1,0:T(8,128)S(1)}, f32[4,8,256]{2,1,0:T(8,128)S(1)}, u32[]{:S(2)}, u32[]{:S(2)}) %collective-permute-start) | collective-permute-done | bytes 32800 | tf_op jit(solution)/shard_map/ppermute | solution.py:329
  9.7 0.2 outer.1
  9.9 0.1 collective-permute-start.1
  10.0 0.0 collective-permute-done.2.theirs_ref
  10.0 0.2 inner_reduce.1
  10.2 0.9 %collective-permute-done.1.theirs_ref = f32[8,128]{1,0:T(8,128)S(1)} collective-permute-done((f32[8,128]{1,0:T(8,128)S(1)}, f32[8,128]{1,0:T(8,128)S(1)}, u32[]{:S(2)}, u32[]{:S(2)}) %collective-permute-start.1) | collective-permute-done | bytes 4128 | tf_op jit(solution)/shard_map/ppermute | solution.py:355
  11.1 0.1 outer_reduce.1
  11.3 9.6 %all_to_all.5.all_ref = f32[8,5,8,256]{3,2,1,0:T(8,128)S(1)} all-to-all(f32[8,5,8,256]{3,2,1,0:T(8,128)S(1)} %broadcast_in_dim.2), channel_id=1, replica_groups={{14,12,10,8,6,4,2,0},{30,28,26,24,22,20,18,16},{15,13,11,9,7,5,3,1},{31..., dimensions={0} | all-to-all | bytes 655360 | tf_op jit(solution)/shard_map/all_to_all | solution.py:378
  21.0 1.1 %collective-permute-start.3 = (f32[5,8,256]{2,1,0:T(8,128)S(1)}, f32[5,8,256]{2,1,0:T(8,128)S(1)}, u32[]{:S(2)}, u32[]{:S(2)}) collective-permute-start(f32[5,8,256]{2,1,0:T(8,128)S(1)} %get-tuple-element.39.mine_ref), channel_id=1, source_target_pairs={{0,16},{2,18},{4,20},{6,22},{8,24},{10,26},{12,28},{14,30},{16,0},... | collective-permute-start | bytes 122888 | tf_op jit(solution)/shard_map/ppermute | solution.py:393
  22.1 3.9 %collective-permute-done.3.theirs_ref = f32[5,8,256]{2,1,0:T(8,128)S(1)} collective-permute-done((f32[5,8,256]{2,1,0:T(8,128)S(1)}, f32[5,8,256]{2,1,0:T(8,128)S(1)}, u32[]{:S(2)}, u32[]{:S(2)}) %collective-permute-start.3) | collective-permute-done | bytes 40992 | tf_op jit(solution)/shard_map/ppermute | solution.py:393
  26.0 0.7 %finish.1 = f32[24,8,256]{2,1,0:T(8,128)} custom-call(f32[2,3,8,256]{3,2,1,0:T(8,128)S(1)} %get-tuple-element.36.outer_ref, f32[21,3,8,256]{3,2,1,0:T(8,128)S(1)} %get-tuple-element.37.inner_ref, f32[5,8,256]{2,1,0:T(8,128)S(1)} %get-tuple-element.39.mine_ref, f32[5,8,256]{2,1,0:T(8,128)S(1)} %collective-permute-done.3.theirs_ref, ...), custom_call_target="tpu_custom_call" | custom-call | tf_op jit(solution)/shard_map/finish/pallas_call | solution.py:402
  (3 shorter events, 0.1 us)
Async XLA Ops:
  0.8 8.9 %collective-permute-start = (f32[4,8,256]{2,1,0:T(8,128)S(1)}, f32[4,8,256]{2,1,0:T(8,128)S(1)}, u32[]{:S(2)}, u32[]{:S(2)}) collective-permute-start(f32[4,8,256]{2,1,0:T(8,128)S(1)} %pad_maximum_fusion), channel_id=1, source_target_pairs={{0,2},{2,4},{4,6},{6,8},{8,10},{10,12},{12,14},{14,16},{16,18},{18... | collective-permute-start | bytes 98312 | tf_op jit(solution)/shard_map/ppermute | solution.py:329
  5.2 4.8 %collective-permute-start.2 = (f32[8,256]{1,0:T(8,128)S(1)}, f32[8,256]{1,0:T(8,128)S(1)}, u32[]{:S(2)}, u32[]{:S(2)}) collective-permute-start(f32[8,256]{1,0:T(8,128)S(1)} %get-tuple-element.34.mine_ref), channel_id=1, source_target_pairs={{0,1},{1,0},{2,3},{3,2},{4,5},{5,4},{6,7},{7,6},{8,9},{9,8},{10,11... | collective-permute-start | bytes 24584 | tf_op jit(solution)/shard_map/ppermute | solution.py:355
  9.9 1.2 %collective-permute-start.1 = (f32[8,128]{1,0:T(8,128)S(1)}, f32[8,128]{1,0:T(8,128)S(1)}, u32[]{:S(2)}, u32[]{:S(2)}) collective-permute-start(f32[8,128]{1,0:T(8,128)S(1)} %get-tuple-element.30.mine_ref), channel_id=1, source_target_pairs={{0,1},{1,0},{2,3},{3,2},{4,5},{5,4},{6,7},{7,6},{8,9},{9,8},{10,11... | collective-permute-start | bytes 12296 | tf_op jit(solution)/shard_map/ppermute | solution.py:355
  21.0 5.0 %collective-permute-start.3 = (f32[5,8,256]{2,1,0:T(8,128)S(1)}, f32[5,8,256]{2,1,0:T(8,128)S(1)}, u32[]{:S(2)}, u32[]{:S(2)}) collective-permute-start(f32[5,8,256]{2,1,0:T(8,128)S(1)} %get-tuple-element.39.mine_ref), channel_id=1, source_target_pairs={{0,16},{2,18},{4,20},{6,22},{8,24},{10,26},{12,28},{14,30},{16,0},... | collective-permute-start | bytes 122888 | tf_op jit(solution)/shard_map/ppermute | solution.py:393
